TPU v7x, 32 devices: a whole 2x2x4 slice. The times are simulated.
32 devices in a mesh: context: 8 (over z, x), dp: 4 (over y, core).
Axes of the slice: x: 2, y: 2, z: 4, core: 2. Of those that a mesh axis runs over, the one named last changes fastest.
Arguments:
- queries: bfloat16 [4, 1024, 1024], P('dp', 'context'), may hold values from -12 to 12
- key_states: bfloat16 [4, 1024, 128], P('dp', 'context'), may hold values from -12 to 12
- value_states: bfloat16 [4, 1024, 128], P('dp', 'context'), may hold values from -6 to 6
- attn_out: bfloat16 [4, 1024, 1024], P('dp', 'context'), may hold values from -6 to 6
- out_grad: bfloat16 [4, 1024, 1024], P('dp', 'context'), may hold values from -6 to 6
- activations: bfloat16 [4, 1024, 8192], P('dp', 'context'), may hold values from -6 to 6
- segment_ids: int32 [4, 1024], P('dp', 'context'), may hold values from 0 to 3, as said below
- span_order: int32 [16], replicated, may hold values from 0 to 15, as said below
- kv_weight: float32 [2, 8192, 128], P(None, ('context', 'dp')), may hold values from -40 to 40
- moment_one: float32 [2, 8192, 128], P(None, ('context', 'dp')), may hold values from -200 to 200
- moment_two: float32 [2, 8192, 128], P(None, ('context', 'dp')), may hold values from 2 to 20000
Outputs:
- query_grad: bfloat16 [4, 1024, 1024], P('dp', 'context')
- kv_grad: bfloat16 [4, 1024, 256], P('dp', 'context')
- new_weight: float32 [2, 8192, 128], P(None, ('context', 'dp'))
- new_moment_one: float32 [2, 8192, 128], P(None, ('context', 'dp'))
- new_moment_two: float32 [2, 8192, 128], P(None, ('context', 'dp'))
- trust_ratio: float32 [2], replicated
Inputs may be any that keep to these rules, and one draw needn't show every extreme that they name: `span_order`: stored spans 2i and 2i+1 hold the sequence's spans p and 15 - p, each span exactly once. `segment_ids`: along positions the ids never fall; every sequence holds ids 0 to 3; the document of the last position holds 8 positions or more.
All inputs are finite; a program needn't handle non-finite values.
Results may differ from a plain program's by a relative error of at most 0.0055.
Values may be sent and summed in bfloat16 or wider, within the bound.
No kernel may reach another device: no remote copies, remote signals or barrier semaphores. Data moves between devices by JAX's collectives and lax.ppermute only.
A program may use at most 64 MiB of HBM per device.

v0:
```python
import jax
import jax.numpy as jnp
from jax import lax
from jax.sharding import PartitionSpec as P

beta_one = 0.9
beta_two = 0.999
epsilon = 1e-06
weight_decay = 0.01
learn_rate = 0.01


def layout_positions(span_order, first_row, row_count, half):
    layout = first_row + jnp.arange(row_count, dtype=jnp.int32)
    which = layout // half
    table = jnp.arange(span_order.shape[0], dtype=jnp.int32)
    picked = jnp.sum(jnp.where(which[:, None] == table[None, :], span_order[None, :], 0), axis=1)
    return picked * half + layout % half


def block_size(total_rows, query_rows):
    block_rows = total_rows
    while block_rows > 4 * query_rows and block_rows % 2 == 0:
        block_rows = block_rows // 2
    return block_rows


def on_device(
    queries,
    key_states,
    value_states,
    attn_out,
    out_grad,
    activations,
    segment_ids,
    span_order,
    kv_weight,
    moment_one,
    moment_two,
):
    device = lax.axis_index("context")
    query_rows = queries.shape[1]
    half = query_rows // 2
    head_dim = key_states.shape[2]
    heads = queries.shape[2] // head_dim
    score_scale = head_dim ** (-0.5)
    query_heads = queries[0].reshape(query_rows, heads, head_dim)
    grad_heads = out_grad[0].reshape(query_rows, heads, head_dim)
    output_heads = attn_out[0].reshape(query_rows, heads, head_dim)
    delta = jnp.sum(grad_heads.astype(jnp.float32) * output_heads.astype(jnp.float32), axis=2)
    query_place = layout_positions(span_order, device * query_rows, query_rows, half)
    query_segment = segment_ids[0]
    all_segments = lax.all_gather(segment_ids, "context", axis=1, tiled=True)[0]

    def visible_for(first_row, row_count):
        key_place = layout_positions(span_order, first_row, row_count, half)
        key_segment = lax.dynamic_slice_in_dim(all_segments, first_row, row_count, 0)
        visible = (key_place[None, :] <= query_place[:, None]) & (
            key_segment[None, :] == query_segment[:, None]
        )
        return visible[:, None, :]

    def score_block(key_block):
        return (
            jnp.einsum("qhd,kd->qhk", query_heads, key_block, preferred_element_type=jnp.float32)
            * score_scale
        )

    seq_length = query_rows * lax.axis_size("context")
    start_stats = (
        jnp.full((query_rows, heads), -1e30, jnp.float32),
        jnp.zeros((query_rows, heads), jnp.float32),
    )
    start_grads = (
        jnp.zeros((query_rows, heads, head_dim), jnp.float32),
        jnp.zeros((seq_length, 2 * head_dim), jnp.float32),
    )
    key_piece = lax.all_gather(key_states, "context", axis=1, tiled=True)
    piece_rows = key_piece.shape[1]
    block_rows = block_size(piece_rows, query_rows)

    def stats_step(block_index, state):
        row_top, row_total = state
        offset = block_index * block_rows
        key_block = lax.dynamic_slice_in_dim(key_piece[0], offset, block_rows, 0)
        visible = visible_for(offset, block_rows)
        scores = score_block(key_block)
        masked = jnp.where(visible, scores, -1e30)
        new_top = jnp.maximum(row_top, jnp.max(masked, axis=2))
        weights = jnp.where(visible, jnp.exp(scores - new_top[:, :, None]), 0.0)
        return (new_top, row_total * jnp.exp(row_top - new_top) + jnp.sum(weights, axis=2))

    row_top, row_total = lax.fori_loop(0, piece_rows // block_rows, stats_step, start_stats)
    log_total = row_top + jnp.log(row_total)
    fold_key_piece = lax.all_gather(key_states, "context", axis=1, tiled=True)
    value_piece = lax.all_gather(value_states, "context", axis=1, tiled=True)
    piece_rows = fold_key_piece.shape[1]
    fold_block_rows = block_size(piece_rows, query_rows)

    def grad_step(block_index, state):
        query_acc, kv_acc = state
        offset = block_index * fold_block_rows
        key_block = lax.dynamic_slice_in_dim(fold_key_piece[0], offset, fold_block_rows, 0)
        value_block = lax.dynamic_slice_in_dim(value_piece[0], offset, fold_block_rows, 0)
        visible = visible_for(offset, fold_block_rows)
        probs = jnp.where(visible, jnp.exp(score_block(key_block) - log_total[:, :, None]), 0.0)
        prob_grad = jnp.einsum(
            "qhd,kd->qhk", grad_heads, value_block, preferred_element_type=jnp.float32
        )
        score_grad = (score_scale * probs * (prob_grad - delta[:, :, None])).astype(jnp.bfloat16)
        query_acc = query_acc + jnp.einsum(
            "qhk,kd->qhd", score_grad, key_block, preferred_element_type=jnp.float32
        )
        key_grad = jnp.einsum(
            "qhk,qhd->kd", score_grad, query_heads, preferred_element_type=jnp.float32
        )
        value_grad = jnp.einsum(
            "qhk,qhd->kd",
            probs.astype(jnp.bfloat16),
            grad_heads,
            preferred_element_type=jnp.float32,
        )
        current = lax.dynamic_slice_in_dim(kv_acc, offset, fold_block_rows, 0)
        summed = current + jnp.concatenate([key_grad, value_grad], axis=1)
        return (query_acc, lax.dynamic_update_slice_in_dim(kv_acc, summed, offset, 0))

    query_acc, kv_acc = lax.fori_loop(0, piece_rows // fold_block_rows, grad_step, start_grads)
    kv_summed = lax.psum_scatter(kv_acc, "context", scatter_dimension=0, tiled=True)
    kv_low = kv_summed.astype(jnp.bfloat16)
    feature_rows = activations[0]
    gradient = lax.psum_scatter(
        lax.dot_general(
            feature_rows, kv_low, (((0,), (0,)), ((), ())), preferred_element_type=jnp.float32
        ),
        ("context", "dp"),
        scatter_dimension=0,
        tiled=True,
    )
    gradient = jnp.stack([gradient[:, :head_dim], gradient[:, head_dim:]])
    new_one = beta_one * moment_one + (1.0 - beta_one) * gradient
    new_two = beta_two * moment_two + (1.0 - beta_two) * gradient * gradient
    update = new_one / (jnp.sqrt(new_two) + epsilon) + weight_decay * kv_weight
    weight_sums, update_sums = lax.psum(
        (jnp.sum(kv_weight * kv_weight, axis=(1, 2)), jnp.sum(update * update, axis=(1, 2))),
        ("context", "dp"),
    )
    trust_ratio = jnp.sqrt(weight_sums) / (jnp.sqrt(update_sums) + epsilon)
    new_weight = kv_weight - learn_rate * trust_ratio[:, None, None] * update
    query_grad = query_acc.reshape(query_rows, heads * head_dim).astype(jnp.bfloat16)
    return (query_grad[None], kv_low[None], new_weight, new_one, new_two, trust_ratio)


def solution(mesh):
    in_specs = (
        P("dp", "context", None),
        P("dp", "context", None),
        P("dp", "context", None),
        P("dp", "context", None),
        P("dp", "context", None),
        P("dp", "context", None),
        P("dp", "context"),
        P(),
        P(None, ("context", "dp"), None),
        P(None, ("context", "dp"), None),
        P(None, ("context", "dp"), None),
    )
    out_specs = (
        P("dp", "context", None),
        P("dp", "context", None),
        P(None, ("context", "dp"), None),
        P(None, ("context", "dp"), None),
        P(None, ("context", "dp"), None),
        P(),
    )
    return jax.shard_map(
        on_device, mesh=mesh, in_specs=in_specs, out_specs=out_specs, check_vma=False
    )
```

profile of v0, /device:TPU:0, one launch (start us, length us, event | category | flops | bytes accessed | tf_op | source)
XLA Modules:
  0.0 404.0 jit_solution(4358770907442450151)
XLA Ops:
  8.2 22.3 %all_gather.10 = s32[1,1024]{1,0:T(1,128)S(1)} all-gather(s32[1,128]{1,0:T(1,128)} %param.21), channel_id=1, replica_groups=mesh['context'=8,'dp'=4] {'context'}, dimensions={1}, use_global_device_ids=true | all-gather | bytes 4608 | tf_op jit(solution)/shard_map/all_gather | solution.py:53
  30.5 33.0 %all_gather.11 = bf16[1,1024,128]{2,1,0:T(8,128)(2,1)} all-gather(bf16[1,128,128]{2,1,0:T(8,128)(2,1)} %param.16), channel_id=1, replica_groups=mesh['context'=8,'dp'=4] {'context'}, dimensions={1}, use_global_device_ids=true | all-gather | bytes 294912 | tf_op jit(solution)/shard_map/all_gather | solution.py:95
  63.4 1.8 copy.40
  66.4 13.0 %while.36 = (s32[]{:T(128)}, f32[128,8]{0,1:T(8,128)S(1)}, f32[128,8]{0,1:T(8,128)S(1)}, s32[16]{0:T(128)}, s32[128]{0:T(128)S(1)}, /*index=5*/s32[1024]{0:T(102...) while((s32[]{:T(128)}, f32[128,8]{0,1:T(8,128)S(1)}, ...), condition=%wide.region_5.6_spmd.clone, body=%wide.region_1.0_spmd.clone.sunk | while | flops 138128896 | bytes 4857102 | solution.py:93
  68.1 2.7 fusion.59
  70.8 2.0 fusion.60
  74.6 2.7 fusion.59
  77.3 2.0 fusion.60
  79.4 32.9 %all_gather.12 = bf16[1,1024,128]{2,1,0:T(8,128)(2,1)} all-gather(bf16[1,128,128]{2,1,0:T(8,128)(2,1)S(1)} %copy-done.13), channel_id=1, replica_groups=mesh['context'=8,'dp'=4] {'context'}, dimensions={1}, use_global_device_ids=true | all-gather | bytes 294912 | tf_op jit(solution)/shard_map/all_gather | solution.py:96
  113.8 27.6 %while.37 = (s32[]{:T(128)}, f32[128,8,128]{2,0,1:T(8,128)}, f32[1024,256]{1,0:T(8,128)}, s32[16]{0:T(128)S(1)}, s32[128]{0:T(128)S(1)}, /*index=5*/s32[1024]{0:...) while((s32[]{:T(128)}, f32[128,8,128]{2,0,1:T(8,128)}, ...), condition=%wide.region_9.10_spmd.clone, body=%wide.region_7.9_spmd.clone.sunk | while | flops 676043264 | bytes 34106796 | solution.py:127
  114.2 1.6 bitcast_select_fusion.3
  117.6 2.3 convolution_add_fusion.2
  120.7 2.0 copy.66
  122.8 2.1 convolution_bitcast_fusion.5
  124.9 1.4 convolution_bitcast_fusion.6
  127.9 1.6 bitcast_select_fusion.3
  131.3 2.5 convolution_add_fusion.2
  134.6 2.0 copy.66
  136.7 2.1 convolution_bitcast_fusion.5
  138.8 1.4 convolution_bitcast_fusion.6
  141.4 60.8 %reduce-scatter.3.cloned.1.call-done = f32[128,256]{1,0:T(8,128)} async-done(((f32[1024,256]{1,0:T(8,128)}), f32[128,256]{1,0:T(8,128)}) %reduce-scatter.3.cloned.1.call-update) | async-done | bytes 131088 | tf_op jit(solution)/shard_map/reduce_scatter | solution.py:128
  202.2 5.4 %convolution_bitcast_fusion.2 = f32[8192,256]{0,1:T(8,128)} fusion(bf16[1,128,8192]{2,1,0:T(8,128)(2,1)S(1)} %copy-done, f32[128,256]{1,0:T(8,128)} %reduce-scatter.3.cloned.1.call-done), kind=kOutput, calls=%fused_computation.60 | convolution fusion | flops 536903680 | bytes 10616832 | tf_op jit(solution)/shard_map/dot_general | solution.py:132
  211.8 144.0 %reduce-scatter.5.cloned.1.call-done = f32[256,256]{0,1:T(8,128)} async-done(((f32[8192,256]{0,1:T(8,128)}), f32[256,256]{0,1:T(8,128)}) %reduce-scatter.5.cloned.1.call-update) | async-done | bytes 262160 | tf_op jit(solution)/shard_map/reduce_scatter | solution.py:131
  358.8 36.8 %all-reduce = (f32[2]{0:T(128)S(1)}, f32[2]{0:T(128)S(1)}) all-reduce(f32[2]{0:T(128)S(1)} %get-tuple-element.696, f32[2]{0:T(128)S(1)} %multiply_reduce_fusion.2), channel_id=1, replica_groups=mesh['context'=8,'dp'=4] {'context','dp'}, use_global_device_ids=true, to_apply=%region_15.16 | all-reduce | flops 4 | bytes 32 | tf_op jit(solution)/shard_map/psum | solution.py:143
  (103 shorter events, 24.0 us)
Async XLA Ops:
  7.2 195.1 %copy-start = (bf16[1,128,8192]{2,1,0:T(8,128)(2,1)S(1)}, bf16[1,128,8192]{2,1,0:T(8,128)(2,1)}, u32[]{:S(2)}) copy-start(bf16[1,128,8192]{2,1,0:T(8,128)(2,1)} %param.20) | copy-start | bytes 6291460
  7.2 195.0 %reduce-scatter.3.cloned.1.call-start = ((), (), s32[]{:S(2)}) async-start(), calls=%async_computation.2 | async-start | bytes 1179648 | tf_op jit(solution)/shard_map/reduce_scatter | solution.py:128
  66.3 13.1 %copy-start.13 = (bf16[1,128,128]{2,1,0:T(8,128)(2,1)S(1)}, bf16[1,128,128]{2,1,0:T(8,128)(2,1)}, u32[]{:S(2)}) copy-start(bf16[1,128,128]{2,1,0:T(8,128)(2,1)} %param.17) | copy-start | bytes 98308
  66.3 46.0 %copy-start.9 = (bf16[1,128,1024]{2,1,0:T(8,128)(2,1)S(1)}, bf16[1,128,1024]{2,1,0:T(8,128)(2,1)}, u32[]{:S(2)}) copy-start(bf16[1,128,1024]{2,1,0:T(8,128)(2,1)} %param.19) | copy-start | bytes 786436
  66.4 46.1 %copy-start.8 = (bf16[1,128,1024]{2,1,0:T(8,128)(2,1)S(1)}, bf16[1,128,1024]{2,1,0:T(8,128)(2,1)}, u32[]{:S(2)}) copy-start(bf16[1,128,1024]{2,1,0:T(8,128)(2,1)} %param.18) | copy-start | bytes 786436
  79.4 34.3 %copy-start.11 = (s32[1,128]{1,0:T(1,128)S(1)}, s32[1,128]{1,0:T(1,128)}, u32[]{:S(2)}) copy-start(s32[1,128]{1,0:T(1,128)} %get-tuple-element.940) | copy-start | bytes 1540
  79.4 34.3 %copy-start.12 = (s32[16]{0:T(128)S(1)}, s32[16]{0:T(128)}, u32[]{:S(2)}) copy-start(s32[16]{0:T(128)} %get-tuple-element.942) | copy-start | bytes 196
  113.8 3.3 copy-start.5
  115.8 1.4 copy-start.1
  117.6 2.3 copy-start.3
  122.8 3.6 copy-start.2
  127.5 3.3 copy-start.5
  129.4 1.4 copy-start.1
  131.2 2.5 copy-start.3
  136.7 3.6 copy-start.2
  141.4 214.5 %reduce-scatter.5.cloned.1.call-start = ((), (), s32[]{:S(2)}) async-start(), calls=%async_computation.3 | async-start | bytes 8650752 | tf_op jit(solution)/shard_map/reduce_scatter | solution.py:131
  207.6 1.0 copy-start.4
  207.6 2.1 copy-start.6
  207.6 2.2 copy-start.10
  207.7 3.6 copy-start.7
Sparse Core Ops, SparseCore 0:
  141.5 60.6 reduce-scatter.2
  207.8 148.0 reduce-scatter.4
where the time goes:
time: 405 us; the launch traced here: 404 us
  waiting for transfers between devices  205 us (51%)
  blocking collectives  125 us (31%)
  matrix products  26.7 us (7%)
  local copies, waits for them, and re-layouts  22 us (5%)
  between operations  14.3 us (4%)
  other arithmetic  10.9 us (3%)
    reduce_scatter x1, waiting for transfers between devices, on_device(): lax.psum_scatter(lax.dot_general(feature_rows, kv_low, (((0,), (0,)), (()...  144 us
    reduce_scatter x1, waiting for transfers between devices, on_device(): lax.psum_scatter(kv_acc, 'context', scatter_dimension=0, tiled=True)  60.8 us
    psum x1, blocking collectives, on_device(): lax.psum((jnp.sum(kv_weight * kv_weight, axis=(1, 2)), jnp.sum(update * u...  36.8 us
    all_gather x1, blocking collectives, on_device(): fold_key_piece = lax.all_gather(key_states, 'context', axis=1, tiled=True)  33 us
    all_gather x1, blocking collectives, on_device(): value_piece = lax.all_gather(value_states, 'context', axis=1, tiled=True)  32.9 us
    all_gather x1, blocking collectives, on_device(): all_segments = lax.all_gather(segment_ids, 'context', axis=1, tiled=True)[0]  22.3 us
    dot_general x4, matrix products, score_block(): jnp.einsum('qhd,kd->qhk', query_heads, key_block, preferred_element_type=...  8.56 us
  transfers between devices with their start and end apart: 2, of which 2 were waited for; matrix products, arithmetic and copies ran while one was open for 1% of the time, Pallas kernels for 0%

commit v1 on v0

--- a/solution.py
+++ b/solution.py
@@ -1,6 +1,10 @@
+import functools
+
 import jax
 import jax.numpy as jnp
 from jax import lax
+from jax.experimental import pallas as pl
+from jax.experimental.pallas import tpu as pltpu
 from jax.sharding import PartitionSpec as P
 
 beta_one = 0.9
@@ -8,6 +12,402 @@
 epsilon = 1e-06
 weight_decay = 0.01
 learn_rate = 0.01
+LOG2E = 1.4426950408889634
+VMEM_LIMIT = 40 * 1024 * 1024
+HIDDEN = -1e30
+ID_ROWS = 16
+
+
+AXES = ("plane", "across", "dp")
+
+
+def xor_permute(value, offset, total):
+    return lax.ppermute(value, AXES, [(i, i ^ offset) for i in range(total)])
+
+
+def local_call(kernel, name, out_shape, in_specs, scratch=(), out_specs=None, **cost):
+    vmem = pl.BlockSpec(memory_space=pltpu.VMEM)
+    return pl.pallas_call(
+        kernel,
+        out_shape=out_shape,
+        in_specs=in_specs,
+        out_specs=[vmem] * len(out_shape) if out_specs is None else out_specs,
+        scratch_shapes=list(scratch),
+        compiler_params=pltpu.CompilerParams(vmem_limit_bytes=VMEM_LIMIT),
+        cost_estimate=pl.CostEstimate(
+            flops=cost.get("flops", 0),
+            bytes_accessed=cost.get("bytes_accessed", 0),
+            transcendentals=cost.get("transcendentals", 0),
+        ),
+        name=name,
+    )
+
+
+VMEM = pl.BlockSpec(memory_space=pltpu.VMEM)
+SMEM = pl.BlockSpec(memory_space=pltpu.SMEM)
+ANYWHERE = pl.BlockSpec(memory_space=pl.ANY)
+
+
+def pack_kernel(key_ref, value_ref, ids_ref, out_ref):
+    rows, head_dim = key_ref.shape
+    out_ref[:rows, :head_dim] = key_ref[...]
+    out_ref[:rows, head_dim:] = value_ref[...]
+    ids = ids_ref[...].astype(jnp.float32).astype(jnp.bfloat16)
+    out_ref[rows:, :rows] = jnp.broadcast_to(ids, (ID_ROWS, rows))
+    out_ref[rows:, rows:] = jnp.zeros((ID_ROWS, 2 * head_dim - rows), jnp.bfloat16)
+
+
+def pack(keys, values, ids):
+    rows, head_dim = keys.shape
+    return local_call(
+        pack_kernel,
+        "pack_keys",
+        [jax.ShapeDtypeStruct((rows + ID_ROWS, 2 * head_dim), jnp.bfloat16)],
+        [VMEM] * 3,
+        bytes_accessed=rows * head_dim * 8,
+    )(keys, values, ids)[0]
+
+
+def prepare_kernel(
+    where_ref, span_ref, q_ref, o_ref, g_ref, q_all, g_all, delta_ref, base_ref, *, heads, half
+):
+    rows = q_ref.shape[0]
+    head_dim = q_ref.shape[1] // heads
+    me = where_ref[0]
+    for head in range(heads):
+        cols = slice(head * head_dim, (head + 1) * head_dim)
+        at = pl.ds(head * rows, rows)
+        grad = g_ref[:, cols]
+        q_all[at, :] = q_ref[:, cols]
+        g_all[at, :] = grad
+        product = grad.astype(jnp.float32) * o_ref[:, cols].astype(jnp.float32)
+        delta_ref[:, at] = jnp.sum(product.T, axis=0, keepdims=True)
+    for piece in range(base_ref.shape[0] // 2):
+        for part in range(2):
+            start = span_ref[2 * (me ^ piece) + part] * half
+            base_ref[2 * piece + part : 2 * piece + part + 1, :] = jnp.full(
+                (1, rows), start, jnp.int32
+            )
+
+
+def prepare(where, span_order, queries, attn_out, out_grad, heads, count):
+    rows, width = queries.shape
+    head_dim = width // heads
+    stacked = jax.ShapeDtypeStruct((heads * rows, head_dim), jnp.bfloat16)
+    return local_call(
+        functools.partial(prepare_kernel, heads=heads, half=rows // 2),
+        "prepare_queries",
+        [
+            stacked,
+            stacked,
+            jax.ShapeDtypeStruct((1, heads * rows), jnp.float32),
+            jax.ShapeDtypeStruct((2 * count, rows), jnp.int32),
+        ],
+        [SMEM, SMEM] + [VMEM] * 3,
+        flops=2 * rows * width,
+        bytes_accessed=10 * rows * width,
+    )(where, span_order, queries, attn_out, out_grad)
+
+
+def attention_kernel(q_all, g_all, delta_ref, base_ref, *refs, pieces, heads, tied):
+    piece_refs = refs[:pieces]
+    refs = refs[pieces + tied :]
+    dq_ref = refs[0]
+    chunk_refs = refs[1 : pieces + 1]
+    k_all, v_all, k_t, bias, probs_t, grads_t = refs[pieces + 1 :]
+    head_dim = q_all.shape[1]
+    rows = q_all.shape[0] // heads
+    half = rows // 2
+    score_scale = head_dim ** (-0.5)
+
+    for piece in range(pieces):
+        at = pl.ds(piece * rows, rows)
+        key = piece_refs[piece][:rows, :head_dim]
+        k_all[at, :] = key
+        v_all[at, :] = piece_refs[piece][:rows, head_dim:]
+        k_t[:, at] = key.T
+
+    segment_rows = [
+        piece_refs[piece][rows : rows + 1, :rows].astype(jnp.float32) for piece in range(pieces)
+    ]
+    all_segments = jnp.concatenate(segment_rows, axis=0)
+    mine = segment_rows[0]
+    first = jnp.zeros((1, rows), jnp.int32)
+    for document in range(1, 4):
+        before = jnp.sum((all_segments < document).astype(jnp.int32))
+        first = jnp.where(mine >= document, before, first)
+    lane = lax.broadcasted_iota(jnp.int32, (1, rows), 1)
+    place = jnp.where(lane < half, base_ref[0:1, :] + lane, base_ref[1:2, :] + lane - half)
+    step = lax.broadcasted_iota(jnp.int32, (half, rows), 0)
+    for part in range(2 * pieces):
+        key_place = base_ref[part : part + 1, :] + step
+        visible = (key_place >= first) & (key_place <= place)
+        bias[pl.ds(part * half, half), :] = jnp.where(visible, 0.0, HIDDEN)
+
+    group = 2
+    width = group * rows
+    for start in range(0, heads, group):
+        at = pl.ds(start * rows, width)
+        contract = (((1,), (1,)), ((), ()))
+        scores = lax.dot_general(
+            k_all[...], q_all[at, :], contract, preferred_element_type=jnp.float32
+        )
+        blocked = bias[...]
+        scores = scores * (score_scale * LOG2E) + jnp.concatenate([blocked] * group, axis=1)
+        top = jnp.max(scores, axis=0, keepdims=True)
+        weights = jnp.exp2(scores - top)
+        probs = weights * (1.0 / jnp.sum(weights, axis=0, keepdims=True))
+        probs_t[:, at] = probs.astype(jnp.bfloat16)
+        prob_grad = lax.dot_general(
+            v_all[...], g_all[at, :], contract, preferred_element_type=jnp.float32
+        )
+        grads_t[:, at] = (score_scale * probs * (prob_grad - delta_ref[:, at])).astype(jnp.bfloat16)
+
+    for piece in range(pieces):
+        at = pl.ds(piece * rows, rows)
+        key_grad = jnp.dot(grads_t[at, :], q_all[...], preferred_element_type=jnp.float32)
+        value_grad = jnp.dot(probs_t[at, :], g_all[...], preferred_element_type=jnp.float32)
+        kept = chunk_refs[piece].dtype
+        chunk_refs[piece][:, :head_dim] = key_grad.astype(kept)
+        chunk_refs[piece][:, head_dim:] = value_grad.astype(kept)
+    for start in range(0, heads, group):
+        at = pl.ds(start * rows, width)
+        query_t = jnp.dot(k_t[...], grads_t[:, at], preferred_element_type=jnp.float32)
+        for head in range(group):
+            block = query_t[:, head * rows : (head + 1) * rows].T
+            cols = pl.ds((start + head) * head_dim, head_dim)
+            dq_ref[:, cols] = block.astype(jnp.bfloat16)
+
+
+def attention(prepared, pieces, tied, heads):
+    stacked, head_dim = prepared[0].shape
+    rows = stacked // heads
+    count = len(pieces)
+    keys = count * rows
+    work = stacked * keys
+    chunk_types = [jnp.float32] + [jnp.bfloat16] * (count - 1)
+    outs = local_call(
+        functools.partial(attention_kernel, pieces=count, heads=heads, tied=len(tied)),
+        "attention_backward",
+        [jax.ShapeDtypeStruct((rows, heads * head_dim), jnp.bfloat16)]
+        + [jax.ShapeDtypeStruct((rows, 2 * head_dim), kind) for kind in chunk_types],
+        [VMEM] * (4 + count) + [ANYWHERE] * len(tied),
+        [
+            pltpu.VMEM((keys, head_dim), jnp.bfloat16),
+            pltpu.VMEM((keys, head_dim), jnp.bfloat16),
+            pltpu.VMEM((head_dim, keys), jnp.bfloat16),
+            pltpu.VMEM((keys, rows), jnp.float32),
+            pltpu.VMEM((keys, stacked), jnp.bfloat16),
+            pltpu.VMEM((keys, stacked), jnp.bfloat16),
+        ],
+        flops=10 * work * head_dim,
+        bytes_accessed=8 * stacked * head_dim,
+        transcendentals=work,
+    )(*prepared, *pieces, *tied)
+    return outs[0], outs[1:]
+
+
+def spread_kernel(where_ref, act_ref, *out_refs, planes, chips, cores, block):
+    plane, chip, core = where_ref[1], where_ref[2], where_ref[3]
+    for offset in range(chips):
+        for other in range(cores):
+            for step in range(planes):
+                owner = ((plane ^ step) * chips + (chip ^ offset)) * cores + (core ^ other)
+                to = (other * planes + step) * block
+                out_refs[offset][:, to : to + block] = act_ref[
+                    :, pl.ds(pl.multiple_of(owner * block, block), block)
+                ]
+
+
+def spread(where, activations, planes, chips, cores):
+    rows, features = activations.shape
+    part = jax.ShapeDtypeStruct((rows, features // chips), activations.dtype)
+    block = features // (planes * chips * cores)
+    return local_call(
+        functools.partial(spread_kernel, planes=planes, chips=chips, cores=cores, block=block),
+        "spread_activations",
+        [part] * chips,
+        [SMEM, VMEM],
+        bytes_accessed=4 * rows * features,
+    )(where, activations)
+
+
+def total_kernel(*refs, count):
+    total = refs[0][...]
+    for ref in refs[1:count]:
+        total = total + ref[...].astype(jnp.float32)
+    refs[-1][...] = total.astype(jnp.bfloat16)
+
+
+def total_kv(terms, tied):
+    return local_call(
+        functools.partial(total_kernel, count=len(terms)),
+        "total_kv",
+        [jax.ShapeDtypeStruct(terms[0].shape, jnp.bfloat16)],
+        [VMEM] * len(terms) + [ANYWHERE] * len(tied),
+        bytes_accessed=terms[0].size * 2 * (len(terms) + 2),
+    )(*terms, *tied)[0]
+
+
+def project_kernel(*refs, chips, half):
+    act_refs, kv_refs = refs[:chips], refs[chips : 2 * chips]
+    own_ref, other_ref, acts = refs[2 * chips :]
+    rows = kv_refs[0].shape[0]
+    for chip in range(chips):
+        acts[pl.ds(chip * rows, rows), :] = act_refs[chip][...]
+    kv_t = jnp.concatenate([ref[...].T for ref in kv_refs], axis=1)
+    other_ref[...] = jnp.dot(
+        kv_t, acts[:, half:], preferred_element_type=jnp.float32
+    ).astype(jnp.bfloat16)
+    own_ref[...] = jnp.dot(kv_t, acts[:, :half], preferred_element_type=jnp.float32)
+
+
+def project(acts, kvs):
+    chips = len(acts)
+    rows, width = kvs[0].shape
+    features = acts[0].shape[1]
+    half = features // 2
+    return local_call(
+        functools.partial(project_kernel, chips=chips, half=half),
+        "project",
+        [
+            jax.ShapeDtypeStruct((width, half), jnp.float32),
+            jax.ShapeDtypeStruct((width, half), jnp.bfloat16),
+        ],
+        [VMEM] * (2 * chips),
+        [pltpu.VMEM((chips * rows, features), jnp.bfloat16)],
+        flops=2 * chips * rows * width * features,
+        bytes_accessed=2 * chips * rows * (features + width),
+    )(*acts, *kvs)
+
+
+def combine_kernel(own_ref, other_ref, *out_refs):
+    block = out_refs[0].shape[1]
+    for step, out_ref in enumerate(out_refs):
+        cols = slice(step * block, (step + 1) * block)
+        total = own_ref[:, cols] + other_ref[:, cols].astype(jnp.float32)
+        out_ref[...] = total.astype(out_ref.dtype)
+
+
+def combine(own, other, planes):
+    width, features = own.shape
+    types = [jnp.float32] + [jnp.bfloat16] * (planes - 1)
+    return local_call(
+        combine_kernel,
+        "combine_cores",
+        [jax.ShapeDtypeStruct((width, features // planes), kind) for kind in types],
+        [VMEM] * 2,
+        bytes_accessed=8 * width * features,
+    )(own, other)
+
+
+def lamb_kernel(*refs, planes):
+    grad_refs = refs[:planes]
+    weight_ref, one_ref, two_ref = refs[planes : planes + 3]
+    new_one_ref, new_two_ref, update_ref, sums_ref = refs[planes + 3 :]
+    total = grad_refs[0][...]
+    for ref in grad_refs[1:]:
+        total = total + ref[...].astype(jnp.float32)
+    gradient = total.T
+    head_dim = weight_ref.shape[2]
+    lane = lax.broadcasted_iota(jnp.int32, sums_ref.shape[1:], 1)
+    sums = jnp.zeros(sums_ref.shape[1:], jnp.float32)
+    for which in range(2):
+        grad = gradient[:, which * head_dim : (which + 1) * head_dim]
+        weight = weight_ref[which]
+        new_one = beta_one * one_ref[which] + (1.0 - beta_one) * grad
+        new_two = beta_two * two_ref[which] + (1.0 - beta_two) * grad * grad
+        update = new_one / (jnp.sqrt(new_two) + epsilon) + weight_decay * weight
+        new_one_ref[which] = new_one
+        new_two_ref[which] = new_two
+        update_ref[which] = update
+        sums = sums + jnp.where(lane == which, jnp.sum(weight * weight), 0.0)
+        sums = sums + jnp.where(lane == 2 + which, jnp.sum(update * update), 0.0)
+    sums_ref[...] = jnp.broadcast_to(sums[None], sums_ref.shape)
+
+
+def lamb(gradients, weight, one, two, total):
+    state = jax.ShapeDtypeStruct(weight.shape, jnp.float32)
+    return local_call(
+        functools.partial(lamb_kernel, planes=len(gradients)),
+        "lamb",
+        [state, state, state, jax.ShapeDtypeStruct((total, 8, 128), jnp.float32)],
+        [VMEM] * (len(gradients) + 3),
+        bytes_accessed=28 * weight.size,
+    )(*gradients, weight, one, two)
+
+
+def finish_kernel(sums_ref, weight_ref, update_ref, new_weight_ref, ratio_ref):
+    sums = jnp.sum(sums_ref[...], axis=0)[0:1, :]
+    lane = lax.broadcasted_iota(jnp.int32, sums.shape, 1)
+
+    def pick(which):
+        return jnp.sum(jnp.where(lane == which, sums, 0.0), axis=1, keepdims=True)
+
+    for which in range(2):
+        ratio = jnp.sqrt(pick(which)) / (jnp.sqrt(pick(2 + which)) + epsilon)
+        new_weight_ref[which] = weight_ref[which] - learn_rate * ratio * update_ref[which]
+        ratio_ref[which] = ratio[0, 0]
+
+
+def finish(sums, weight, update):
+    return local_call(
+        finish_kernel,
+        "finish",
+        [
+            jax.ShapeDtypeStruct(weight.shape, jnp.float32),
+            jax.ShapeDtypeStruct((2,), jnp.float32),
+        ],
+        [VMEM] * 3,
+        out_specs=[VMEM, SMEM],
+        bytes_accessed=12 * weight.size,
+    )(sums, weight, update)
+
+
+def on_device_small(
+    queries,
+    key_states,
+    value_states,
+    attn_out,
+    out_grad,
+    activations,
+    segment_ids,
+    span_order,
+    kv_weight,
+    moment_one,
+    moment_two,
+):
+    cores = 2
+    dp_count = lax.axis_size("dp")
+    planes = lax.axis_size("plane")
+    places = lax.axis_size("across") * dp_count
+    chips = places // cores
+    total = planes * places
+    count = total // dp_count
+    heads = queries.shape[2] // key_states.shape[2]
+    linear = lax.axis_index(AXES)
+    where = jnp.stack(
+        [linear // dp_count, linear // places, linear % places // cores, linear % cores]
+    ).astype(jnp.int32)
+
+    own = pack(key_states[0], value_states[0], segment_ids)
+    pieces = [own] + [xor_permute(own, m * dp_count, total) for m in range(1, count)]
+    parts = spread(where, activations[0], planes, chips, cores)
+    acts = [parts[0]] + [xor_permute(parts[m], m * cores, total) for m in range(1, chips)]
+    prepared = prepare(where, span_order, queries[0], attn_out[0], out_grad[0], heads, count)
+
+    query_grad, chunks = attention(prepared, pieces, acts[1:-1], heads)
+    terms = [chunks[0]] + [xor_permute(chunks[m], m * dp_count, total) for m in range(1, count)]
+    kv_low = total_kv(terms, acts[-1:])
+
+    kvs = [kv_low] + [xor_permute(kv_low, m * cores, total) for m in range(1, chips)]
+    partial, sent = project(acts, kvs)
+    blocks = combine(partial, xor_permute(sent, 1, total), planes)
+    gradients = [blocks[0]] + [xor_permute(blocks[m], m * places, total) for m in range(1, planes)]
+    new_one, new_two, update, sums = lamb(gradients, kv_weight, moment_one, moment_two, total)
+    sums = lax.all_to_all(sums, AXES, split_axis=0, concat_axis=0)
+    new_weight, ratios = finish(sums, kv_weight, update)
+    return (query_grad[None], kv_low[None], new_weight, new_one, new_two, ratios)
 
 
 def layout_positions(span_order, first_row, row_count, half):
@@ -76,6 +476,7 @@
         jnp.zeros((seq_length, 2 * head_dim), jnp.float32),
     )
     key_piece = lax.all_gather(key_states, "context", axis=1, tiled=True)
+    value_piece = lax.all_gather(value_states, "context", axis=1, tiled=True)
     piece_rows = key_piece.shape[1]
     block_rows = block_size(piece_rows, query_rows)
 
@@ -92,17 +493,13 @@
 
     row_top, row_total = lax.fori_loop(0, piece_rows // block_rows, stats_step, start_stats)
     log_total = row_top + jnp.log(row_total)
-    fold_key_piece = lax.all_gather(key_states, "context", axis=1, tiled=True)
-    value_piece = lax.all_gather(value_states, "context", axis=1, tiled=True)
-    piece_rows = fold_key_piece.shape[1]
-    fold_block_rows = block_size(piece_rows, query_rows)
 
     def grad_step(block_index, state):
         query_acc, kv_acc = state
-        offset = block_index * fold_block_rows
-        key_block = lax.dynamic_slice_in_dim(fold_key_piece[0], offset, fold_block_rows, 0)
-        value_block = lax.dynamic_slice_in_dim(value_piece[0], offset, fold_block_rows, 0)
-        visible = visible_for(offset, fold_block_rows)
+        offset = block_index * block_rows
+        key_block = lax.dynamic_slice_in_dim(key_piece[0], offset, block_rows, 0)
+        value_block = lax.dynamic_slice_in_dim(value_piece[0], offset, block_rows, 0)
+        visible = visible_for(offset, block_rows)
         probs = jnp.where(visible, jnp.exp(score_block(key_block) - log_total[:, :, None]), 0.0)
         prob_grad = jnp.einsum(
             "qhd,kd->qhk", grad_heads, value_block, preferred_element_type=jnp.float32
@@ -120,11 +517,11 @@
             grad_heads,
             preferred_element_type=jnp.float32,
         )
-        current = lax.dynamic_slice_in_dim(kv_acc, offset, fold_block_rows, 0)
+        current = lax.dynamic_slice_in_dim(kv_acc, offset, block_rows, 0)
         summed = current + jnp.concatenate([key_grad, value_grad], axis=1)
         return (query_acc, lax.dynamic_update_slice_in_dim(kv_acc, summed, offset, 0))
 
-    query_acc, kv_acc = lax.fori_loop(0, piece_rows // fold_block_rows, grad_step, start_grads)
+    query_acc, kv_acc = lax.fori_loop(0, piece_rows // block_rows, grad_step, start_grads)
     kv_summed = lax.psum_scatter(kv_acc, "context", scatter_dimension=0, tiled=True)
     kv_low = kv_summed.astype(jnp.bfloat16)
     feature_rows = activations[0]
@@ -172,6 +569,26 @@
         P(None, ("context", "dp"), None),
         P(),
     )
+    if mesh.shape["context"] == 8 and mesh.shape["dp"] == 4:
+        split = jax.sharding.Mesh(mesh.devices.reshape(4, 2, 4), AXES)
+        context = AXES[:2]
+
+        def renamed(specs):
+            return tuple(
+                P(*[
+                    context if name == "context" else AXES if isinstance(name, tuple) else name
+                    for name in spec
+                ])
+                for spec in specs
+            )
+
+        return jax.shard_map(
+            on_device_small,
+            mesh=split,
+            in_specs=renamed(in_specs),
+            out_specs=renamed(out_specs),
+            check_vma=False,
+        )
     return jax.shard_map(
         on_device, mesh=mesh, in_specs=in_specs, out_specs=out_specs, check_vma=False
     )

time: 405 us -> 99.2 us (0.24)
  waiting for transfers between devices: 205 us -> 36.8 us
  blocking collectives: 125 us -> 12.2 us
  starting transfers between devices: 0.08 us -> 36.7 us
  matrix products: 26.7 us -> 0 us
  local copies, waits for them, and re-layouts: 22 us -> 2.47 us
  between operations: 14.3 us -> 0.81 us
  other arithmetic: 10.9 us -> 0.08 us
  Pallas kernels: 0 us -> 9.92 us
    reduce_scatter x2 -> x0, waiting for transfers between devices: 205 us -> none  [the longest x1 144 us: on_device(): lax.psum_scatter(lax.dot_general(feature_rows, kv_low, (((0,), (0,)), (()...]
    all_gather x3 -> x0, blocking collectives: 88.1 us -> none  [the longest x1 33 us: on_device(): fold_key_piece = lax.all_gather(key_states, 'context', axis=1, tiled=True)]
    psum x1 -> x0, blocking collectives: 36.8 us -> none  [on_device(): lax.psum((jnp.sum(kv_weight * kv_weight, axis=(1, 2)), jnp.sum(update * u...]
    ppermute x0 -> x24, waiting for transfers between devices: none -> 36.8 us  [xor_permute(): return lax.ppermute(value, AXES, [(i, i ^ offset) for i in range(total)])]
    ppermute x0 -> x24, starting transfers between devices: none -> 36.7 us  [xor_permute(): return lax.ppermute(value, AXES, [(i, i ^ offset) for i in range(total)])]
    dot_general x13 -> x0, matrix products: 26.7 us -> none  [the longest x4 8.56 us: score_block(): jnp.einsum('qhd,kd->qhk', query_heads, key_block, preferred_element_type=...]
    all_to_all x0 -> x1, blocking collectives: none -> 12.2 us  [on_device_small(): sums = lax.all_to_all(sums, AXES, split_axis=0, concat_axis=0)]
    pallas_call x0 -> x9, Pallas kernels: none -> 9.92 us  [the longest x1 4.87 us: attention(): local_call(functools.partial(attention_kernel, pieces=count, heads=heads,...]
  transfers between devices with their start and end apart: 2 -> 24, of which waited for: 2 -> 12; matrix products, arithmetic and copies ran while one was open for 1% -> 0% of each run, Pallas kernels for 0% -> 6%
where the time goes in v1:
time: 99.2 us; the launch traced here: 99 us
  waiting for transfers between devices  36.8 us (37%)
  starting transfers between devices  36.7 us (37%)
  blocking collectives  12.2 us (12%)
  Pallas kernels  9.92 us (10%)
  local copies, waits for them, and re-layouts  2.47 us (2%)
    ppermute x24, waiting for transfers between devices, xor_permute(): return lax.ppermute(value, AXES, [(i, i ^ offset) for i in range(total)])  36.8 us
    ppermute x24, starting transfers between devices, xor_permute(): return lax.ppermute(value, AXES, [(i, i ^ offset) for i in range(total)])  36.7 us
    all_to_all x1, blocking collectives, on_device_small(): sums = lax.all_to_all(sums, AXES, split_axis=0, concat_axis=0)  12.2 us
    pallas_call x1, Pallas kernels, attention(): local_call(functools.partial(attention_kernel, pieces=count, heads=heads,...  4.87 us
    unnamed x24, local copies, waits for them, and re-layouts  2.47 us
  transfers between devices with their start and end apart: 24, of which 12 were waited for; matrix products, arithmetic and copies ran while one was open for 0% of the time, Pallas kernels for 6%

profile of v1, /device:TPU:0, one launch (start us, length us, event | category | flops | bytes accessed | tf_op | source)
XLA Modules:
  0.0 99.0 jit_solution(7895513854607100510)
XLA Ops:
  0.8 1.6 %copy-done = bf16[1,128,8192]{2,1,0:T(8,128)(2,1)S(1)} copy-done((bf16[1,128,8192]{2,1,0:T(8,128)(2,1)S(1)}, bf16[1,128,8192]{2,1,0:T(8,128)(2,1)}, u32[]{:S(2)}) %copy-start) | copy-done | bytes 2097176
  3.2 3.0 %collective-permute-start.7 = (bf16[128,2048]{1,0:T(8,128)(2,1)S(1)}, bf16[128,2048]{1,0:T(8,128)(2,1)S(1)}, u32[]{:S(2)}, u32[]{:S(2)}) collective-permute-start(bf16[128,2048]{1,0:T(8,128)(2,1)S(1)} %get-tuple-element.39), channel_id=1, source_target_pairs={{0,2},{1,3},{2,0},{3,1},{4,6},{5,7},{6,4},{7,5},{8,10},{9,11},{10,... | collective-permute-start | bytes 1572872 | tf_op jit(solution)/shard_map/ppermute | solution.py:25
  7.9 5.0 %collective-permute-start.6 = (bf16[144,256]{1,0:T(8,128)(2,1)S(1)}, bf16[144,256]{1,0:T(8,128)(2,1)S(1)}, u32[]{:S(2)}, u32[]{:S(2)}) collective-permute-start(bf16[144,256]{1,0:T(8,128)(2,1)S(1)} %pack_keys.1.refs_0_), channel_id=1, source_target_pairs={{0,28},{1,29},{2,30},{3,31},{4,24},{5,25},{6,26},{7,27},{8,20},{9,... | collective-permute-start | bytes 221192 | tf_op jit(solution)/shard_map/ppermute | solution.py:25
  13.1 2.3 %collective-permute-done.6.refs_7_ = bf16[144,256]{1,0:T(8,128)(2,1)S(1)} collective-permute-done((bf16[144,256]{1,0:T(8,128)(2,1)S(1)}, bf16[144,256]{1,0:T(8,128)(2,1)S(1)}, u32[]{:S(2)}, u32[]{:S(2)}) %collective-permute-start.6) | collective-permute-done | bytes 73760 | tf_op jit(solution)/shard_map/ppermute | solution.py:25
  15.4 5.7 %collective-permute-start.4 = (bf16[144,256]{1,0:T(8,128)(2,1)S(1)}, bf16[144,256]{1,0:T(8,128)(2,1)S(1)}, u32[]{:S(2)}, u32[]{:S(2)}) collective-permute-start(bf16[144,256]{1,0:T(8,128)(2,1)S(1)} %pack_keys.1.refs_0_), channel_id=1, source_target_pairs={{0,20},{1,21},{2,22},{3,23},{4,16},{5,17},{6,18},{7,19},{8,28},{9,... | collective-permute-start | bytes 221192 | tf_op jit(solution)/shard_map/ppermute | solution.py:25
  22.0 2.3 %collective-permute-done.4.refs_5_ = bf16[144,256]{1,0:T(8,128)(2,1)S(1)} collective-permute-done((bf16[144,256]{1,0:T(8,128)(2,1)S(1)}, bf16[144,256]{1,0:T(8,128)(2,1)S(1)}, u32[]{:S(2)}, u32[]{:S(2)}) %collective-permute-start.4) | collective-permute-done | bytes 73760 | tf_op jit(solution)/shard_map/ppermute | solution.py:25
  24.6 1.8 %collective-permute-done.3.refs_4_ = bf16[144,256]{1,0:T(8,128)(2,1)S(1)} collective-permute-done((bf16[144,256]{1,0:T(8,128)(2,1)S(1)}, bf16[144,256]{1,0:T(8,128)(2,1)S(1)}, u32[]{:S(2)}, u32[]{:S(2)}) %collective-permute-start.3) | collective-permute-done | bytes 73760 | tf_op jit(solution)/shard_map/ppermute | solution.py:25
  26.5 3.2 %collective-permute-done.2.refs_3_ = bf16[144,256]{1,0:T(8,128)(2,1)S(1)} collective-permute-done((bf16[144,256]{1,0:T(8,128)(2,1)S(1)}, bf16[144,256]{1,0:T(8,128)(2,1)S(1)}, u32[]{:S(2)}, u32[]{:S(2)}) %collective-permute-start.2) | collective-permute-done | bytes 73760 | tf_op jit(solution)/shard_map/ppermute | solution.py:25
  31.2 6.0 %collective-permute-done.refs_1_ = bf16[144,256]{1,0:T(8,128)(2,1)S(1)} collective-permute-done((bf16[144,256]{1,0:T(8,128)(2,1)S(1)}, bf16[144,256]{1,0:T(8,128)(2,1)S(1)}, u32[]{:S(2)}, u32[]{:S(2)}) %collective-permute-start) | collective-permute-done | bytes 73760 | tf_op jit(solution)/shard_map/ppermute | solution.py:25
  37.2 4.9 %attention_backward.1 = (bf16[128,1024]{1,0:T(8,128)(2,1)}, f32[128,256]{1,0:T(8,128)S(1)}, bf16[128,256]{1,0:T(8,128)(2,1)S(1)}, bf16[128,256]{1,0:T(8,128)(2,1...) custom-call(bf16[1024,128]{1,0:T(8,128)(2,1)S(1)} %get-tuple-element, ...), custom_call_target="tpu_custom_call" | custom-call | flops 1342177280 | bytes 1048576 | tf_op jit(solution)/shard_map/attention_backward/pallas_call | solution.py:189
  42.1 1.5 %collective-permute-start.9 = (bf16[128,256]{1,0:T(8,128)(2,1)S(1)}, bf16[128,256]{1,0:T(8,128)(2,1)S(1)}, u32[]{:S(2)}, u32[]{:S(2)}) collective-permute-start(bf16[128,256]{1,0:T(8,128)(2,1)S(1)} %get-tuple-element.43), channel_id=1, source_target_pairs={{0,4},{1,5},{2,6},{3,7},{4,0},{5,1},{6,2},{7,3},{8,12},{9,13},{10,... | collective-permute-start | bytes 196616 | tf_op jit(solution)/shard_map/ppermute | solution.py:25
  43.6 1.6 %collective-permute-start.10 = (bf16[128,256]{1,0:T(8,128)(2,1)S(1)}, bf16[128,256]{1,0:T(8,128)(2,1)S(1)}, u32[]{:S(2)}, u32[]{:S(2)}) collective-permute-start(bf16[128,256]{1,0:T(8,128)(2,1)S(1)} %get-tuple-element.44), channel_id=1, source_target_pairs={{0,8},{1,9},{2,10},{3,11},{4,12},{5,13},{6,14},{7,15},{8,0},{9,1},... | collective-permute-start | bytes 196616 | tf_op jit(solution)/shard_map/ppermute | solution.py:25
  45.6 2.6 %collective-permute-start.12 = (bf16[128,256]{1,0:T(8,128)(2,1)S(1)}, bf16[128,256]{1,0:T(8,128)(2,1)S(1)}, u32[]{:S(2)}, u32[]{:S(2)}) collective-permute-start(bf16[128,256]{1,0:T(8,128)(2,1)S(1)} %get-tuple-element.46), channel_id=1, source_target_pairs={{0,16},{1,17},{2,18},{3,19},{4,20},{5,21},{6,22},{7,23},{8,24},{9,... | collective-permute-start | bytes 196616 | tf_op jit(solution)/shard_map/ppermute | solution.py:25
  49.5 3.6 %collective-permute-start.14 = (bf16[128,256]{1,0:T(8,128)(2,1)S(1)}, bf16[128,256]{1,0:T(8,128)(2,1)S(1)}, u32[]{:S(2)}, u32[]{:S(2)}) collective-permute-start(bf16[128,256]{1,0:T(8,128)(2,1)S(1)} %get-tuple-element.48), channel_id=1, source_target_pairs={{0,24},{1,25},{2,26},{3,27},{4,28},{5,29},{6,30},{7,31},{8,16},{9,... | collective-permute-start | bytes 196616 | tf_op jit(solution)/shard_map/ppermute | solution.py:25
  53.2 4.8 %collective-permute-done.13.refs_5_ = bf16[128,256]{1,0:T(8,128)(2,1)S(1)} collective-permute-done((bf16[128,256]{1,0:T(8,128)(2,1)S(1)}, bf16[128,256]{1,0:T(8,128)(2,1)S(1)}, u32[]{:S(2)}, u32[]{:S(2)}) %collective-permute-start.13) | collective-permute-done | bytes 65568 | tf_op jit(solution)/shard_map/ppermute | solution.py:25
  58.0 2.1 %collective-permute-done.15.refs_7_ = bf16[128,256]{1,0:T(8,128)(2,1)S(1)} collective-permute-done((bf16[128,256]{1,0:T(8,128)(2,1)S(1)}, bf16[128,256]{1,0:T(8,128)(2,1)S(1)}, u32[]{:S(2)}, u32[]{:S(2)}) %collective-permute-start.15) | collective-permute-done | bytes 65568 | tf_op jit(solution)/shard_map/ppermute | solution.py:25
  61.3 1.5 %collective-permute-start.18 = (bf16[128,256]{1,0:T(8,128)(2,1)}, bf16[128,256]{1,0:T(8,128)(2,1)S(1)}, u32[]{:S(2)}, u32[]{:S(2)}) collective-permute-start(bf16[128,256]{1,0:T(8,128)(2,1)} %total_kv.1.refs_4_), channel_id=1, source_target_pairs={{0,4},{1,5},{2,6},{3,7},{4,0},{5,1},{6,2},{7,3},{8,12},{9,13},{10,... | collective-permute-start | bytes 196616 | tf_op jit(solution)/shard_map/ppermute | solution.py:25
  62.8 1.5 %collective-permute-start.17 = (bf16[128,256]{1,0:T(8,128)(2,1)}, bf16[128,256]{1,0:T(8,128)(2,1)S(1)}, u32[]{:S(2)}, u32[]{:S(2)}) collective-permute-start(bf16[128,256]{1,0:T(8,128)(2,1)} %total_kv.1.refs_4_), channel_id=1, source_target_pairs={{0,2},{1,3},{2,0},{3,1},{4,6},{5,7},{6,4},{7,5},{8,10},{9,11},{10,... | collective-permute-start | bytes 196616 | tf_op jit(solution)/shard_map/ppermute | solution.py:25
  64.3 1.9 %collective-permute-done.19.refs_7_ = bf16[128,256]{1,0:T(8,128)(2,1)S(1)} collective-permute-done((bf16[128,256]{1,0:T(8,128)(2,1)}, bf16[128,256]{1,0:T(8,128)(2,1)S(1)}, u32[]{:S(2)}, u32[]{:S(2)}) %collective-permute-start.19) | collective-permute-done | bytes 65568 | tf_op jit(solution)/shard_map/ppermute | solution.py:25
  68.9 1.9 %collective-permute-done.20.other_ref = bf16[256,1024]{1,0:T(8,128)(2,1)S(1)} collective-permute-done((bf16[256,1024]{1,0:T(8,128)(2,1)S(1)}, bf16[256,1024]{1,0:T(8,128)(2,1)S(1)}, u32[]{:S(2)}, u32[]{:S(2)}) %collective-permute-start.20) | collective-permute-done | bytes 524320 | tf_op jit(solution)/shard_map/ppermute | solution.py:25
  72.6 2.8 %collective-permute-start.23 = (bf16[256,256]{1,0:T(8,128)(2,1)S(1)}, bf16[256,256]{1,0:T(8,128)(2,1)S(1)}, u32[]{:S(2)}, u32[]{:S(2)}) collective-permute-start(bf16[256,256]{1,0:T(8,128)(2,1)S(1)} %get-tuple-element.57), channel_id=1, source_target_pairs={{0,24},{1,25},{2,26},{3,27},{4,28},{5,29},{6,30},{7,31},{8,16},{9,... | collective-permute-start | bytes 393224 | tf_op jit(solution)/shard_map/ppermute | solution.py:25
  75.4 3.1 %collective-permute-done.21.refs_1_ = bf16[256,256]{1,0:T(8,128)(2,1)S(1)} collective-permute-done((bf16[256,256]{1,0:T(8,128)(2,1)S(1)}, bf16[256,256]{1,0:T(8,128)(2,1)S(1)}, u32[]{:S(2)}, u32[]{:S(2)}) %collective-permute-start.21) | collective-permute-done | bytes 131104 | tf_op jit(solution)/shard_map/ppermute | solution.py:25
  78.5 6.3 %collective-permute-done.22.refs_2_ = bf16[256,256]{1,0:T(8,128)(2,1)S(1)} collective-permute-done((bf16[256,256]{1,0:T(8,128)(2,1)S(1)}, bf16[256,256]{1,0:T(8,128)(2,1)S(1)}, u32[]{:S(2)}, u32[]{:S(2)}) %collective-permute-start.22) | collective-permute-done | bytes 131104 | tf_op jit(solution)/shard_map/ppermute | solution.py:25
  85.9 12.2 %all_to_all.5.sums_ref = f32[32,8,128]{2,1,0:T(8,128)S(1)} all-to-all(f32[32,8,128]{2,1,0:T(8,128)S(1)} %get-tuple-element.58), channel_id=1, replica_groups=mesh['plane'=4,'across'=2,'dp'=4] {'plane','across','dp'}, dimensions={0} | all-to-all | bytes 262144 | tf_op jit(solution)/shard_map/all_to_all | solution.py:408
  (59 shorter events, 14.9 us)
Async XLA Ops:
  3.2 34.0 %collective-permute-start.7 = (bf16[128,2048]{1,0:T(8,128)(2,1)S(1)}, bf16[128,2048]{1,0:T(8,128)(2,1)S(1)}, u32[]{:S(2)}, u32[]{:S(2)}) collective-permute-start(bf16[128,2048]{1,0:T(8,128)(2,1)S(1)} %get-tuple-element.39), channel_id=1, source_target_pairs={{0,2},{1,3},{2,0},{3,1},{4,6},{5,7},{6,4},{7,5},{8,10},{9,11},{10,... | collective-permute-start | bytes 1572872 | tf_op jit(solution)/shard_map/ppermute | solution.py:25
  6.3 30.9 %collective-permute-start.8 = (bf16[128,2048]{1,0:T(8,128)(2,1)S(1)}, bf16[128,2048]{1,0:T(8,128)(2,1)S(1)}, u32[]{:S(2)}, u32[]{:S(2)}) collective-permute-start(bf16[128,2048]{1,0:T(8,128)(2,1)S(1)} %get-tuple-element.40), channel_id=1, source_target_pairs={{0,4},{1,5},{2,6},{3,7},{4,0},{5,1},{6,2},{7,3},{8,12},{9,13},{10,... | collective-permute-start | bytes 1572872 | tf_op jit(solution)/shard_map/ppermute | solution.py:25
  7.8 40.4 %collective-permute-start.16 = (bf16[128,2048]{1,0:T(8,128)(2,1)S(1)}, bf16[128,2048]{1,0:T(8,128)(2,1)S(1)}, u32[]{:S(2)}, u32[]{:S(2)}) collective-permute-start(bf16[128,2048]{1,0:T(8,128)(2,1)S(1)} %get-tuple-element.50), channel_id=1, source_target_pairs={{0,6},{1,7},{2,4},{3,5},{4,2},{5,3},{6,0},{7,1},{8,14},{9,15},{10,... | collective-permute-start | bytes 1572872 | tf_op jit(solution)/shard_map/ppermute | solution.py:25
  7.9 7.5 %collective-permute-start.6 = (bf16[144,256]{1,0:T(8,128)(2,1)S(1)}, bf16[144,256]{1,0:T(8,128)(2,1)S(1)}, u32[]{:S(2)}, u32[]{:S(2)}) collective-permute-start(bf16[144,256]{1,0:T(8,128)(2,1)S(1)} %pack_keys.1.refs_0_), channel_id=1, source_target_pairs={{0,28},{1,29},{2,30},{3,31},{4,24},{5,25},{6,26},{7,27},{8,20},{9,... | collective-permute-start | bytes 221192 | tf_op jit(solution)/shard_map/ppermute | solution.py:25
  12.9 8.2 %collective-permute-start.5 = (bf16[144,256]{1,0:T(8,128)(2,1)S(1)}, bf16[144,256]{1,0:T(8,128)(2,1)S(1)}, u32[]{:S(2)}, u32[]{:S(2)}) collective-permute-start(bf16[144,256]{1,0:T(8,128)(2,1)S(1)} %pack_keys.1.refs_0_), channel_id=1, source_target_pairs={{0,24},{1,25},{2,26},{3,27},{4,28},{5,29},{6,30},{7,31},{8,16},{9,... | collective-permute-start | bytes 221192 | tf_op jit(solution)/shard_map/ppermute | solution.py:25
  15.4 9.0 %collective-permute-start.4 = (bf16[144,256]{1,0:T(8,128)(2,1)S(1)}, bf16[144,256]{1,0:T(8,128)(2,1)S(1)}, u32[]{:S(2)}, u32[]{:S(2)}) collective-permute-start(bf16[144,256]{1,0:T(8,128)(2,1)S(1)} %pack_keys.1.refs_0_), channel_id=1, source_target_pairs={{0,20},{1,21},{2,22},{3,23},{4,16},{5,17},{6,18},{7,19},{8,28},{9,... | collective-permute-start | bytes 221192 | tf_op jit(solution)/shard_map/ppermute | solution.py:25
  21.1 5.4 %collective-permute-start.3 = (bf16[144,256]{1,0:T(8,128)(2,1)S(1)}, bf16[144,256]{1,0:T(8,128)(2,1)S(1)}, u32[]{:S(2)}, u32[]{:S(2)}) collective-permute-start(bf16[144,256]{1,0:T(8,128)(2,1)S(1)} %pack_keys.1.refs_0_), channel_id=1, source_target_pairs={{0,16},{1,17},{2,18},{3,19},{4,20},{5,21},{6,22},{7,23},{8,24},{9,... | collective-permute-start | bytes 221192 | tf_op jit(solution)/shard_map/ppermute | solution.py:25
  24.3 5.4 %collective-permute-start.2 = (bf16[144,256]{1,0:T(8,128)(2,1)S(1)}, bf16[144,256]{1,0:T(8,128)(2,1)S(1)}, u32[]{:S(2)}, u32[]{:S(2)}) collective-permute-start(bf16[144,256]{1,0:T(8,128)(2,1)S(1)} %pack_keys.1.refs_0_), channel_id=1, source_target_pairs={{0,12},{1,13},{2,14},{3,15},{4,8},{5,9},{6,10},{7,11},{8,4},{9,5},... | collective-permute-start | bytes 221192 | tf_op jit(solution)/shard_map/ppermute | solution.py:25
  26.5 4.7 %collective-permute-start.1 = (bf16[144,256]{1,0:T(8,128)(2,1)S(1)}, bf16[144,256]{1,0:T(8,128)(2,1)S(1)}, u32[]{:S(2)}, u32[]{:S(2)}) collective-permute-start(bf16[144,256]{1,0:T(8,128)(2,1)S(1)} %pack_keys.1.refs_0_), channel_id=1, source_target_pairs={{0,8},{1,9},{2,10},{3,11},{4,12},{5,13},{6,14},{7,15},{8,0},{9,1},... | collective-permute-start | bytes 221192 | tf_op jit(solution)/shard_map/ppermute | solution.py:25
  29.7 7.5 %collective-permute-start = (bf16[144,256]{1,0:T(8,128)(2,1)S(1)}, bf16[144,256]{1,0:T(8,128)(2,1)S(1)}, u32[]{:S(2)}, u32[]{:S(2)}) collective-permute-start(bf16[144,256]{1,0:T(8,128)(2,1)S(1)} %pack_keys.1.refs_0_), channel_id=1, source_target_pairs={{0,4},{1,5},{2,6},{3,7},{4,0},{5,1},{6,2},{7,3},{8,12},{9,13},{10,... | collective-permute-start | bytes 221192 | tf_op jit(solution)/shard_map/ppermute | solution.py:25
  42.1 7.4 %collective-permute-start.9 = (bf16[128,256]{1,0:T(8,128)(2,1)S(1)}, bf16[128,256]{1,0:T(8,128)(2,1)S(1)}, u32[]{:S(2)}, u32[]{:S(2)}) collective-permute-start(bf16[128,256]{1,0:T(8,128)(2,1)S(1)} %get-tuple-element.43), channel_id=1, source_target_pairs={{0,4},{1,5},{2,6},{3,7},{4,0},{5,1},{6,2},{7,3},{8,12},{9,13},{10,... | collective-permute-start | bytes 196616 | tf_op jit(solution)/shard_map/ppermute | solution.py:25
  43.6 9.5 %collective-permute-start.10 = (bf16[128,256]{1,0:T(8,128)(2,1)S(1)}, bf16[128,256]{1,0:T(8,128)(2,1)S(1)}, u32[]{:S(2)}, u32[]{:S(2)}) collective-permute-start(bf16[128,256]{1,0:T(8,128)(2,1)S(1)} %get-tuple-element.44), channel_id=1, source_target_pairs={{0,8},{1,9},{2,10},{3,11},{4,12},{5,13},{6,14},{7,15},{8,0},{9,1},... | collective-permute-start | bytes 196616 | tf_op jit(solution)/shard_map/ppermute | solution.py:25
  45.2 8.1 %collective-permute-start.11 = (bf16[128,256]{1,0:T(8,128)(2,1)S(1)}, bf16[128,256]{1,0:T(8,128)(2,1)S(1)}, u32[]{:S(2)}, u32[]{:S(2)}) collective-permute-start(bf16[128,256]{1,0:T(8,128)(2,1)S(1)} %get-tuple-element.45), channel_id=1, source_target_pairs={{0,12},{1,13},{2,14},{3,15},{4,8},{5,9},{6,10},{7,11},{8,4},{9,5},... | collective-permute-start | bytes 196616 | tf_op jit(solution)/shard_map/ppermute | solution.py:25
  45.6 7.7 %collective-permute-start.12 = (bf16[128,256]{1,0:T(8,128)(2,1)S(1)}, bf16[128,256]{1,0:T(8,128)(2,1)S(1)}, u32[]{:S(2)}, u32[]{:S(2)}) collective-permute-start(bf16[128,256]{1,0:T(8,128)(2,1)S(1)} %get-tuple-element.46), channel_id=1, source_target_pairs={{0,16},{1,17},{2,18},{3,19},{4,20},{5,21},{6,22},{7,23},{8,24},{9,... | collective-permute-start | bytes 196616 | tf_op jit(solution)/shard_map/ppermute | solution.py:25
  48.2 9.8 %collective-permute-start.13 = (bf16[128,256]{1,0:T(8,128)(2,1)S(1)}, bf16[128,256]{1,0:T(8,128)(2,1)S(1)}, u32[]{:S(2)}, u32[]{:S(2)}) collective-permute-start(bf16[128,256]{1,0:T(8,128)(2,1)S(1)} %get-tuple-element.47), channel_id=1, source_target_pairs={{0,20},{1,21},{2,22},{3,23},{4,16},{5,17},{6,18},{7,19},{8,28},{9,... | collective-permute-start | bytes 196616 | tf_op jit(solution)/shard_map/ppermute | solution.py:25
  49.5 8.6 %collective-permute-start.14 = (bf16[128,256]{1,0:T(8,128)(2,1)S(1)}, bf16[128,256]{1,0:T(8,128)(2,1)S(1)}, u32[]{:S(2)}, u32[]{:S(2)}) collective-permute-start(bf16[128,256]{1,0:T(8,128)(2,1)S(1)} %get-tuple-element.48), channel_id=1, source_target_pairs={{0,24},{1,25},{2,26},{3,27},{4,28},{5,29},{6,30},{7,31},{8,16},{9,... | collective-permute-start | bytes 196616 | tf_op jit(solution)/shard_map/ppermute | solution.py:25
  53.1 7.1 %collective-permute-start.15 = (bf16[128,256]{1,0:T(8,128)(2,1)S(1)}, bf16[128,256]{1,0:T(8,128)(2,1)S(1)}, u32[]{:S(2)}, u32[]{:S(2)}) collective-permute-start(bf16[128,256]{1,0:T(8,128)(2,1)S(1)} %get-tuple-element.49), channel_id=1, source_target_pairs={{0,28},{1,29},{2,30},{3,31},{4,24},{5,25},{6,26},{7,27},{8,20},{9,... | collective-permute-start | bytes 196616 | tf_op jit(solution)/shard_map/ppermute | solution.py:25
  60.8 5.4 %collective-permute-start.19 = (bf16[128,256]{1,0:T(8,128)(2,1)}, bf16[128,256]{1,0:T(8,128)(2,1)S(1)}, u32[]{:S(2)}, u32[]{:S(2)}) collective-permute-start(bf16[128,256]{1,0:T(8,128)(2,1)} %total_kv.1.refs_4_), channel_id=1, source_target_pairs={{0,6},{1,7},{2,4},{3,5},{4,2},{5,3},{6,0},{7,1},{8,14},{9,15},{10,... | collective-permute-start | bytes 196616 | tf_op jit(solution)/shard_map/ppermute | solution.py:25
  61.3 4.9 %collective-permute-start.18 = (bf16[128,256]{1,0:T(8,128)(2,1)}, bf16[128,256]{1,0:T(8,128)(2,1)S(1)}, u32[]{:S(2)}, u32[]{:S(2)}) collective-permute-start(bf16[128,256]{1,0:T(8,128)(2,1)} %total_kv.1.refs_4_), channel_id=1, source_target_pairs={{0,4},{1,5},{2,6},{3,7},{4,0},{5,1},{6,2},{7,3},{8,12},{9,13},{10,... | collective-permute-start | bytes 196616 | tf_op jit(solution)/shard_map/ppermute | solution.py:25
  62.8 4.5 %collective-permute-start.17 = (bf16[128,256]{1,0:T(8,128)(2,1)}, bf16[128,256]{1,0:T(8,128)(2,1)S(1)}, u32[]{:S(2)}, u32[]{:S(2)}) collective-permute-start(bf16[128,256]{1,0:T(8,128)(2,1)} %total_kv.1.refs_4_), channel_id=1, source_target_pairs={{0,2},{1,3},{2,0},{3,1},{4,6},{5,7},{6,4},{7,5},{8,10},{9,11},{10,... | collective-permute-start | bytes 196616 | tf_op jit(solution)/shard_map/ppermute | solution.py:25
  68.8 2.0 %collective-permute-start.20 = (bf16[256,1024]{1,0:T(8,128)(2,1)S(1)}, bf16[256,1024]{1,0:T(8,128)(2,1)S(1)}, u32[]{:S(2)}, u32[]{:S(2)}) collective-permute-start(bf16[256,1024]{1,0:T(8,128)(2,1)S(1)} %get-tuple-element.53), channel_id=1, source_target_pairs={{0,1},{1,0},{2,3},{3,2},{4,5},{5,4},{6,7},{7,6},{8,9},{9,8},{10,11... | collective-permute-start | bytes 1572872 | tf_op jit(solution)/shard_map/ppermute | solution.py:25
  70.9 7.6 %collective-permute-start.21 = (bf16[256,256]{1,0:T(8,128)(2,1)S(1)}, bf16[256,256]{1,0:T(8,128)(2,1)S(1)}, u32[]{:S(2)}, u32[]{:S(2)}) collective-permute-start(bf16[256,256]{1,0:T(8,128)(2,1)S(1)} %get-tuple-element.55), channel_id=1, source_target_pairs={{0,8},{1,9},{2,10},{3,11},{4,12},{5,13},{6,14},{7,15},{8,0},{9,1},... | collective-permute-start | bytes 393224 | tf_op jit(solution)/shard_map/ppermute | solution.py:25
  71.9 12.9 %collective-permute-start.22 = (bf16[256,256]{1,0:T(8,128)(2,1)S(1)}, bf16[256,256]{1,0:T(8,128)(2,1)S(1)}, u32[]{:S(2)}, u32[]{:S(2)}) collective-permute-start(bf16[256,256]{1,0:T(8,128)(2,1)S(1)} %get-tuple-element.56), channel_id=1, source_target_pairs={{0,16},{1,17},{2,18},{3,19},{4,20},{5,21},{6,22},{7,23},{8,24},{9,... | collective-permute-start | bytes 393224 | tf_op jit(solution)/shard_map/ppermute | solution.py:25
  72.6 12.3 %collective-permute-start.23 = (bf16[256,256]{1,0:T(8,128)(2,1)S(1)}, bf16[256,256]{1,0:T(8,128)(2,1)S(1)}, u32[]{:S(2)}, u32[]{:S(2)}) collective-permute-start(bf16[256,256]{1,0:T(8,128)(2,1)S(1)} %get-tuple-element.57), channel_id=1, source_target_pairs={{0,24},{1,25},{2,26},{3,27},{4,28},{5,29},{6,30},{7,31},{8,16},{9,... | collective-permute-start | bytes 393224 | tf_op jit(solution)/shard_map/ppermute | solution.py:25
  (12 other events, 211.3 us)

commit v2 on v1

--- a/solution.py
+++ b/solution.py
@@ -14,6 +14,7 @@
 learn_rate = 0.01
 LOG2E = 1.4426950408889634
 VMEM_LIMIT = 40 * 1024 * 1024
+VMEM_MOST = 60 * 1024 * 1024
 HIDDEN = -1e30
 ID_ROWS = 16
 
@@ -21,11 +22,16 @@
 AXES = ("plane", "across", "dp")
 
 
+def my_place():
+    dp = lax.axis_index("dp")
+    return lax.axis_index("plane"), lax.axis_index("across"), dp // 2, dp % 2
+
+
 def xor_permute(value, offset, total):
     return lax.ppermute(value, AXES, [(i, i ^ offset) for i in range(total)])
 
 
-def local_call(kernel, name, out_shape, in_specs, scratch=(), out_specs=None, **cost):
+def local_call(kernel, name, out_shape, in_specs, scratch=(), out_specs=None, limit=None, **cost):
     vmem = pl.BlockSpec(memory_space=pltpu.VMEM)
     return pl.pallas_call(
         kernel,
@@ -33,7 +39,7 @@
         in_specs=in_specs,
         out_specs=[vmem] * len(out_shape) if out_specs is None else out_specs,
         scratch_shapes=list(scratch),
-        compiler_params=pltpu.CompilerParams(vmem_limit_bytes=VMEM_LIMIT),
+        compiler_params=pltpu.CompilerParams(vmem_limit_bytes=limit or VMEM_LIMIT),
         cost_estimate=pl.CostEstimate(
             flops=cost.get("flops", 0),
             bytes_accessed=cost.get("bytes_accessed", 0),
@@ -48,7 +54,7 @@
 ANYWHERE = pl.BlockSpec(memory_space=pl.ANY)
 
 
-def pack_kernel(key_ref, value_ref, ids_ref, out_ref):
+def write_piece(key_ref, value_ref, ids_ref, out_ref):
     rows, head_dim = key_ref.shape
     out_ref[:rows, :head_dim] = key_ref[...]
     out_ref[:rows, head_dim:] = value_ref[...]
@@ -57,23 +63,93 @@
     out_ref[rows:, rows:] = jnp.zeros((ID_ROWS, 2 * head_dim - rows), jnp.bfloat16)
 
 
-def pack(keys, values, ids):
+def pack_kernel(
+    key_ref, value_ref, ids_ref, act_ref, out_ref, sent_ref, piece, ids, stage, sems, *, block
+):
+    rows, head_dim = key_ref.shape
+    wide = 2 * block
+    count = sent_ref.shape[1] // wide
+    other = 1 - my_place()[2]
+    small = [
+        pltpu.make_async_copy(key_ref, piece.at[:rows, :head_dim], sems.at[2 * count]),
+        pltpu.make_async_copy(value_ref, piece.at[:rows, head_dim:], sems.at[2 * count + 1]),
+        pltpu.make_async_copy(ids_ref, ids, sems.at[2 * count + 2]),
+    ]
+    arriving, leaving = [], []
+    for index in range(count):
+        start = pl.multiple_of((2 * index + other) * wide, wide)
+        to = pl.ds(index * wide, wide)
+        arriving.append(
+            pltpu.make_async_copy(
+                act_ref.at[:, pl.ds(start, wide)], stage.at[:, to], sems.at[index]
+            )
+        )
+        leaving.append(
+            pltpu.make_async_copy(stage.at[:, to], sent_ref.at[:, to], sems.at[count + index])
+        )
+    for copy in small + arriving:
+        copy.start()
+    for copy in small:
+        copy.wait()
+    low = ids[...].astype(jnp.float32).astype(jnp.bfloat16)
+    piece[rows:, :rows] = jnp.broadcast_to(low, (ID_ROWS, rows))
+    piece[rows:, rows:] = jnp.zeros((ID_ROWS, 2 * head_dim - rows), jnp.bfloat16)
+    result = pltpu.make_async_copy(piece, out_ref, sems.at[2 * count + 3])
+    result.start()
+    for here, there in zip(arriving, leaving):
+        here.wait()
+        there.start()
+    for copy in leaving:
+        copy.wait()
+    result.wait()
+
+
+def pack(keys, values, ids, activations, block):
     rows, head_dim = keys.shape
-    return local_call(
-        pack_kernel,
-        "pack_keys",
-        [jax.ShapeDtypeStruct((rows + ID_ROWS, 2 * head_dim), jnp.bfloat16)],
-        [VMEM] * 3,
-        bytes_accessed=rows * head_dim * 8,
-    )(keys, values, ids)[0]
+    half = activations.shape[1] // 2
+    packed = (rows + ID_ROWS, 2 * head_dim)
+    return local_call(
+        functools.partial(pack_kernel, block=block),
+        "pack",
+        [
+            jax.ShapeDtypeStruct(packed, jnp.bfloat16),
+            jax.ShapeDtypeStruct((rows, half), jnp.bfloat16),
+        ],
+        [ANYWHERE] * 4,
+        [
+            pltpu.VMEM(packed, jnp.bfloat16),
+            pltpu.VMEM(ids.shape, jnp.int32),
+            pltpu.VMEM((rows, half), jnp.bfloat16),
+            pltpu.SemaphoreType.DMA((half // block + 4,)),
+        ],
+        out_specs=[ANYWHERE] * 2,
+        limit=VMEM_MOST,
+        bytes_accessed=4 * rows * half,
+    )(keys, values, ids, activations)
 
 
 def prepare_kernel(
-    where_ref, span_ref, q_ref, o_ref, g_ref, q_all, g_all, delta_ref, base_ref, *, heads, half
+    span_ref,
+    key_ref,
+    value_ref,
+    ids_ref,
+    q_ref,
+    o_ref,
+    g_ref,
+    piece_ref,
+    q_all,
+    g_all,
+    delta_ref,
+    base_ref,
+    *,
+    heads,
+    half,
 ):
+    write_piece(key_ref, value_ref, ids_ref, piece_ref)
     rows = q_ref.shape[0]
     head_dim = q_ref.shape[1] // heads
-    me = where_ref[0]
+    plane, across, _, _ = my_place()
+    me = 2 * plane + across
     for head in range(heads):
         cols = slice(head * head_dim, (head + 1) * head_dim)
         at = pl.ds(head * rows, rows)
@@ -90,7 +166,7 @@
             )
 
 
-def prepare(where, span_order, queries, attn_out, out_grad, heads, count):
+def prepare(span_order, keys, values, ids, queries, attn_out, out_grad, heads, count):
     rows, width = queries.shape
     head_dim = width // heads
     stacked = jax.ShapeDtypeStruct((heads * rows, head_dim), jnp.bfloat16)
@@ -98,23 +174,21 @@
         functools.partial(prepare_kernel, heads=heads, half=rows // 2),
         "prepare_queries",
         [
+            jax.ShapeDtypeStruct((rows + ID_ROWS, 2 * head_dim), jnp.bfloat16),
             stacked,
             stacked,
             jax.ShapeDtypeStruct((1, heads * rows), jnp.float32),
             jax.ShapeDtypeStruct((2 * count, rows), jnp.int32),
         ],
-        [SMEM, SMEM] + [VMEM] * 3,
+        [SMEM] + [VMEM] * 6,
         flops=2 * rows * width,
         bytes_accessed=10 * rows * width,
-    )(where, span_order, queries, attn_out, out_grad)
-
-
-def attention_kernel(q_all, g_all, delta_ref, base_ref, *refs, pieces, heads, tied):
+    )(span_order, keys, values, ids, queries, attn_out, out_grad)
+
+
+def attention_kernel(q_all, g_all, delta_ref, base_ref, *refs, pieces, heads):
     piece_refs = refs[:pieces]
-    refs = refs[pieces + tied :]
-    dq_ref = refs[0]
-    chunk_refs = refs[1 : pieces + 1]
-    k_all, v_all, k_t, bias, probs_t, grads_t = refs[pieces + 1 :]
+    probs_t, grads_t, k_t, k_all, v_all, bias = refs[pieces:]
     head_dim = q_all.shape[1]
     rows = q_all.shape[0] // heads
     half = rows // 2
@@ -163,15 +237,62 @@
         )
         grads_t[:, at] = (score_scale * probs * (prob_grad - delta_ref[:, at])).astype(jnp.bfloat16)
 
-    for piece in range(pieces):
-        at = pl.ds(piece * rows, rows)
-        key_grad = jnp.dot(grads_t[at, :], q_all[...], preferred_element_type=jnp.float32)
-        value_grad = jnp.dot(probs_t[at, :], g_all[...], preferred_element_type=jnp.float32)
-        kept = chunk_refs[piece].dtype
-        chunk_refs[piece][:, :head_dim] = key_grad.astype(kept)
-        chunk_refs[piece][:, head_dim:] = value_grad.astype(kept)
+
+def attention(prepared, pieces, heads):
+    stacked, head_dim = prepared[0].shape
+    rows = stacked // heads
+    keys = len(pieces) * rows
+    work = stacked * keys
+    square = jax.ShapeDtypeStruct((keys, stacked), jnp.bfloat16)
+    return local_call(
+        functools.partial(attention_kernel, pieces=len(pieces), heads=heads),
+        "attention_scores",
+        [square, square, jax.ShapeDtypeStruct((head_dim, keys), jnp.bfloat16)],
+        [VMEM] * (4 + len(pieces)),
+        [
+            pltpu.VMEM((keys, head_dim), jnp.bfloat16),
+            pltpu.VMEM((keys, head_dim), jnp.bfloat16),
+            pltpu.VMEM((keys, rows), jnp.float32),
+        ],
+        flops=4 * work * head_dim,
+        bytes_accessed=4 * work,
+        transcendentals=work,
+    )(*prepared, *pieces)
+
+
+def terms_kernel(probs_t, grads_t, q_all, g_all, *refs, groups, rows):
+    out_refs = refs[-len(groups) :]
+    head_dim = q_all.shape[1]
+    for out_ref, group in zip(out_refs, groups):
+        for index, piece in enumerate(group):
+            at = pl.ds(piece * rows, rows)
+            to = pl.ds(index * rows, rows)
+            key_grad = jnp.dot(grads_t[at, :], q_all[...], preferred_element_type=jnp.float32)
+            value_grad = jnp.dot(probs_t[at, :], g_all[...], preferred_element_type=jnp.float32)
+            out_ref[to, :head_dim] = key_grad.astype(out_ref.dtype)
+            out_ref[to, head_dim:] = value_grad.astype(out_ref.dtype)
+
+
+def kv_terms(probs_t, grads_t, q_all, g_all, tied, groups, kind, rows):
+    keys, stacked = probs_t.shape
+    head_dim = q_all.shape[1]
+    return local_call(
+        functools.partial(terms_kernel, groups=groups, rows=rows),
+        "kv_terms",
+        [jax.ShapeDtypeStruct((len(group) * rows, 2 * head_dim), kind) for group in groups],
+        [VMEM] * 4 + [ANYWHERE] * len(tied),
+        flops=2 * keys * stacked * head_dim,
+        bytes_accessed=2 * keys * stacked,
+    )(probs_t, grads_t, q_all, g_all, *tied)
+
+
+def query_kernel(k_t, grads_t, dq_ref, mark_ref, *, heads):
+    mark_ref[...] = jnp.zeros_like(mark_ref)
+    head_dim = k_t.shape[0]
+    rows = grads_t.shape[1] // heads
+    group = 2
     for start in range(0, heads, group):
-        at = pl.ds(start * rows, width)
+        at = pl.ds(start * rows, group * rows)
         query_t = jnp.dot(k_t[...], grads_t[:, at], preferred_element_type=jnp.float32)
         for head in range(group):
             block = query_t[:, head * rows : (head + 1) * rows].T
@@ -179,63 +300,42 @@
             dq_ref[:, cols] = block.astype(jnp.bfloat16)
 
 
-def attention(prepared, pieces, tied, heads):
-    stacked, head_dim = prepared[0].shape
-    rows = stacked // heads
-    count = len(pieces)
-    keys = count * rows
-    work = stacked * keys
-    chunk_types = [jnp.float32] + [jnp.bfloat16] * (count - 1)
-    outs = local_call(
-        functools.partial(attention_kernel, pieces=count, heads=heads, tied=len(tied)),
-        "attention_backward",
-        [jax.ShapeDtypeStruct((rows, heads * head_dim), jnp.bfloat16)]
-        + [jax.ShapeDtypeStruct((rows, 2 * head_dim), kind) for kind in chunk_types],
-        [VMEM] * (4 + count) + [ANYWHERE] * len(tied),
+def query_gradient(k_t, grads_t, heads):
+    head_dim, keys = k_t.shape
+    stacked = grads_t.shape[1]
+    return local_call(
+        functools.partial(query_kernel, heads=heads),
+        "query_gradient",
         [
-            pltpu.VMEM((keys, head_dim), jnp.bfloat16),
-            pltpu.VMEM((keys, head_dim), jnp.bfloat16),
-            pltpu.VMEM((head_dim, keys), jnp.bfloat16),
-            pltpu.VMEM((keys, rows), jnp.float32),
-            pltpu.VMEM((keys, stacked), jnp.bfloat16),
-            pltpu.VMEM((keys, stacked), jnp.bfloat16),
+            jax.ShapeDtypeStruct((stacked // heads, heads * head_dim), jnp.bfloat16),
+            jax.ShapeDtypeStruct((8, 128), jnp.float32),
         ],
-        flops=10 * work * head_dim,
-        bytes_accessed=8 * stacked * head_dim,
-        transcendentals=work,
-    )(*prepared, *pieces, *tied)
-    return outs[0], outs[1:]
-
-
-def spread_kernel(where_ref, act_ref, *out_refs, planes, chips, cores, block):
-    plane, chip, core = where_ref[1], where_ref[2], where_ref[3]
-    for offset in range(chips):
-        for other in range(cores):
-            for step in range(planes):
-                owner = ((plane ^ step) * chips + (chip ^ offset)) * cores + (core ^ other)
-                to = (other * planes + step) * block
-                out_refs[offset][:, to : to + block] = act_ref[
-                    :, pl.ds(pl.multiple_of(owner * block, block), block)
-                ]
-
-
-def spread(where, activations, planes, chips, cores):
-    rows, features = activations.shape
-    part = jax.ShapeDtypeStruct((rows, features // chips), activations.dtype)
-    block = features // (planes * chips * cores)
-    return local_call(
-        functools.partial(spread_kernel, planes=planes, chips=chips, cores=cores, block=block),
-        "spread_activations",
-        [part] * chips,
-        [SMEM, VMEM],
-        bytes_accessed=4 * rows * features,
-    )(where, activations)
+        [VMEM] * 2,
+        flops=2 * keys * stacked * head_dim,
+        bytes_accessed=2 * keys * stacked,
+    )(k_t, grads_t)
+
+
+def chunk_groups(planes):
+    return [
+        [(core, across, step) for core in range(2) for across in range(2)]
+        for step in reversed(range(planes))
+    ]
+
+
+def chunk_starts(place, offsets, block):
+    core, across, step = offsets
+    chip = (place[0] ^ step) * 2 + (place[1] ^ across)
+    core = place[3] ^ core
+    own = ((2 * chip + place[2]) * 2 + core) * block
+    return pl.multiple_of(own, block), pl.multiple_of((2 * chip + core) * block, block)
 
 
 def total_kernel(*refs, count):
     total = refs[0][...]
     for ref in refs[1:count]:
         total = total + ref[...].astype(jnp.float32)
+    refs[-2][...] = total
     refs[-1][...] = total.astype(jnp.bfloat16)
 
 
@@ -243,62 +343,65 @@
     return local_call(
         functools.partial(total_kernel, count=len(terms)),
         "total_kv",
-        [jax.ShapeDtypeStruct(terms[0].shape, jnp.bfloat16)],
+        [jax.ShapeDtypeStruct(terms[0].shape, kind) for kind in (jnp.float32, jnp.bfloat16)],
         [VMEM] * len(terms) + [ANYWHERE] * len(tied),
-        bytes_accessed=terms[0].size * 2 * (len(terms) + 2),
-    )(*terms, *tied)[0]
-
-
-def project_kernel(*refs, chips, half):
-    act_refs, kv_refs = refs[:chips], refs[chips : 2 * chips]
-    own_ref, other_ref, acts = refs[2 * chips :]
-    rows = kv_refs[0].shape[0]
-    for chip in range(chips):
-        acts[pl.ds(chip * rows, rows), :] = act_refs[chip][...]
-    kv_t = jnp.concatenate([ref[...].T for ref in kv_refs], axis=1)
-    other_ref[...] = jnp.dot(
-        kv_t, acts[:, half:], preferred_element_type=jnp.float32
-    ).astype(jnp.bfloat16)
-    own_ref[...] = jnp.dot(kv_t, acts[:, :half], preferred_element_type=jnp.float32)
-
-
-def project(acts, kvs):
-    chips = len(acts)
+        bytes_accessed=terms[0].size * 2 * (len(terms) + 3),
+    )(*terms, *tied)
+
+
+def project_kernel(
+    own_ref, other_ref, own_kv, other_kv, *refs, chunks, block
+):
+    keep_ref, send_ref = refs[-2:]
+    place = my_place()
+    kv_t = jnp.concatenate([own_kv[...].T, other_kv[...].T], axis=1)
+    half = len(chunks) // 2
+    for index, offsets in enumerate(chunks):
+        own_start, other_start = chunk_starts(place, offsets, block)
+        acts = jnp.concatenate(
+            [own_ref[:, pl.ds(own_start, block)], other_ref[:, pl.ds(other_start, block)]], axis=0
+        )
+        part = jnp.dot(kv_t, acts, preferred_element_type=jnp.float32)
+        out_ref = keep_ref if index < half else send_ref
+        out_ref[:, pl.ds(index % half * block, block)] = part.astype(out_ref.dtype)
+
+
+def project(own, other, kvs, tied, chunks, block):
     rows, width = kvs[0].shape
-    features = acts[0].shape[1]
-    half = features // 2
-    return local_call(
-        functools.partial(project_kernel, chips=chips, half=half),
+    kept = len(chunks) // 2 * block
+    return local_call(
+        functools.partial(project_kernel, chunks=chunks, block=block),
         "project",
         [
-            jax.ShapeDtypeStruct((width, half), jnp.float32),
-            jax.ShapeDtypeStruct((width, half), jnp.bfloat16),
+            jax.ShapeDtypeStruct((width, kept), jnp.float32),
+            jax.ShapeDtypeStruct((width, kept), jnp.bfloat16),
         ],
-        [VMEM] * (2 * chips),
-        [pltpu.VMEM((chips * rows, features), jnp.bfloat16)],
-        flops=2 * chips * rows * width * features,
-        bytes_accessed=2 * chips * rows * (features + width),
-    )(*acts, *kvs)
-
-
-def combine_kernel(own_ref, other_ref, *out_refs):
-    block = out_refs[0].shape[1]
+        [VMEM] * 4 + [ANYWHERE] * len(tied),
+        flops=8 * rows * width * kept,
+        bytes_accessed=4 * rows * kept,
+    )(own, other, *kvs, *tied)
+
+
+def combine_kernel(own_ref, other_ref, *refs, tied, axis):
+    out_refs = refs[tied:]
+    size = out_refs[0].shape[axis]
     for step, out_ref in enumerate(out_refs):
-        cols = slice(step * block, (step + 1) * block)
-        total = own_ref[:, cols] + other_ref[:, cols].astype(jnp.float32)
+        part = pl.ds(step * size, size)
+        at = (part, slice(None)) if axis == 0 else (slice(None), part)
+        total = own_ref[at] + other_ref[at].astype(jnp.float32)
         out_ref[...] = total.astype(out_ref.dtype)
 
 
-def combine(own, other, planes):
-    width, features = own.shape
-    types = [jnp.float32] + [jnp.bfloat16] * (planes - 1)
-    return local_call(
-        combine_kernel,
-        "combine_cores",
-        [jax.ShapeDtypeStruct((width, features // planes), kind) for kind in types],
-        [VMEM] * 2,
-        bytes_accessed=8 * width * features,
-    )(own, other)
+def combine(own, other, types, axis, tied=()):
+    shape = list(own.shape)
+    shape[axis] //= len(types)
+    return local_call(
+        functools.partial(combine_kernel, tied=len(tied), axis=axis),
+        "combine",
+        [jax.ShapeDtypeStruct(tuple(shape), kind) for kind in types],
+        [VMEM] * 2 + [ANYWHERE] * len(tied),
+        bytes_accessed=8 * own.size,
+    )(own, other, *tied)
 
 
 def lamb_kernel(*refs, planes):
@@ -377,32 +480,53 @@
     moment_one,
     moment_two,
 ):
-    cores = 2
-    dp_count = lax.axis_size("dp")
+    core, up, across = 1, 2, lax.axis_size("dp")
     planes = lax.axis_size("plane")
-    places = lax.axis_size("across") * dp_count
-    chips = places // cores
+    places = lax.axis_size("across") * across
     total = planes * places
-    count = total // dp_count
+    count = total // across
     heads = queries.shape[2] // key_states.shape[2]
-    linear = lax.axis_index(AXES)
-    where = jnp.stack(
-        [linear // dp_count, linear // places, linear % places // cores, linear % cores]
-    ).astype(jnp.int32)
-
-    own = pack(key_states[0], value_states[0], segment_ids)
-    pieces = [own] + [xor_permute(own, m * dp_count, total) for m in range(1, count)]
-    parts = spread(where, activations[0], planes, chips, cores)
-    acts = [parts[0]] + [xor_permute(parts[m], m * cores, total) for m in range(1, chips)]
-    prepared = prepare(where, span_order, queries[0], attn_out[0], out_grad[0], heads, count)
-
-    query_grad, chunks = attention(prepared, pieces, acts[1:-1], heads)
-    terms = [chunks[0]] + [xor_permute(chunks[m], m * dp_count, total) for m in range(1, count)]
-    kv_low = total_kv(terms, acts[-1:])
-
-    kvs = [kv_low] + [xor_permute(kv_low, m * cores, total) for m in range(1, chips)]
-    partial, sent = project(acts, kvs)
-    blocks = combine(partial, xor_permute(sent, 1, total), planes)
+    block = kv_weight.shape[1]
+    keys, values = key_states[0], value_states[0]
+    low, full = jnp.bfloat16, jnp.float32
+
+    own, acts = pack(keys, values, segment_ids, activations[0], block)
+    other_acts = xor_permute(acts, up, total)
+    level = [own] + [xor_permute(own, m * places, total) for m in range(1, planes)]
+    passed = [xor_permute(piece, across, total) for piece in level]
+    piece, *prepared = prepare(
+        span_order, keys, values, segment_ids, queries[0], attn_out[0], out_grad[0], heads, count
+    )
+    pieces = [piece for pair in zip([piece] + level[1:], passed) for piece in pair]
+
+    probs_t, grads_t, k_t = attention(prepared, pieces, heads)
+    squares = (probs_t, grads_t, prepared[0], prepared[1])
+    rows = keys.shape[0]
+    sent, after = {}, []
+    for step in reversed(range(planes)):
+        after = kv_terms(*squares, after, [[2 * step + 1]], low, rows)
+        [sent[step]] = after
+    kept = kv_terms(*squares, after, [[2 * step] for step in range(planes)], full, rows)
+    query_grad, mark = query_gradient(k_t, grads_t, heads)
+    terms = []
+    for step in range(planes):
+        kind = full if step == 0 else low
+        terms += combine(kept[step], xor_permute(sent[step], across, total), [kind], 0)
+    terms = [terms[0]] + [xor_permute(terms[m], m * places, total) for m in range(1, planes)]
+    kv_sum, kv_sent = total_kv(terms, [other_acts, mark])
+    kv_low = kv_sum.astype(low)
+
+    kvs = [kv_sent, xor_permute(kv_sent, up, total)]
+    blocks, after = {}, []
+    for group in chunk_groups(planes):
+        step = group[0][2]
+        keep, send = project(activations[0], other_acts, kvs, [], group, block)
+        keep, send = combine(keep, xor_permute(send, core, total), [full, low], 1, after)
+        after = [send]
+        if step == planes // 2:
+            after = [send, blocks[planes - 1]]
+        kind = full if step == 0 else low
+        [blocks[step]] = combine(keep, xor_permute(send, across, total), [kind], 1)
     gradients = [blocks[0]] + [xor_permute(blocks[m], m * places, total) for m in range(1, planes)]
     new_one, new_two, update, sums = lamb(gradients, kv_weight, moment_one, moment_two, total)
     sums = lax.all_to_all(sums, AXES, split_axis=0, concat_axis=0)

time: 99.2 us -> 79.4 us (0.80)
  blocking collectives: 12.2 us -> 0 us
  waiting for transfers between devices: 36.8 us -> 31.4 us
  starting transfers between devices: 36.7 us -> 33.7 us
  Pallas kernels: 9.92 us -> 12.5 us
  local copies, waits for them, and re-layouts: 2.47 us -> 0.05 us
    ppermute x24 -> x27, waiting for transfers between devices: 36.8 us -> 23.8 us  [xor_permute(): return lax.ppermute(value, AXES, [(i, i ^ offset) for i in range(total)])]
    all_to_all x1 -> x0, blocking collectives: 12.2 us -> none  [on_device_small(): sums = lax.all_to_all(sums, AXES, split_axis=0, concat_axis=0)]
    all_to_all x0 -> x1, waiting for transfers between devices: none -> 7.59 us  [on_device_small(): sums = lax.all_to_all(sums, AXES, split_axis=0, concat_axis=0)]
    ppermute x24 -> x27, starting transfers between devices: 36.7 us -> 30.3 us  [xor_permute(): return lax.ppermute(value, AXES, [(i, i ^ offset) for i in range(total)])]
    all_to_all x0 -> x1, starting transfers between devices: none -> 3.35 us  [on_device_small(): sums = lax.all_to_all(sums, AXES, split_axis=0, concat_axis=0)]
    pallas_call x5 -> x24, Pallas kernels: 6.54 us -> 9.75 us  [the longest x1 2.73 us: attention(): local_call(functools.partial(attention_kernel, pieces=len(pieces), heads=...]
    unnamed x24 -> x22, local copies, waits for them, and re-layouts: 2.47 us -> 0.05 us
  transfers between devices with their start and end apart: 24 -> 28, of which waited for: 12 -> 12; matrix products, arithmetic and copies ran while one was open for 0% -> 1% of each run, Pallas kernels for 6% -> 10%
where the time goes in v2:
time: 79.4 us; the launch traced here: 79.2 us
  starting transfers between devices  33.7 us (42%)
  waiting for transfers between devices  31.4 us (40%)
  Pallas kernels  12.5 us (16%)
  between operations  0.96 us (1%)
    ppermute x27, starting transfers between devices, xor_permute(): return lax.ppermute(value, AXES, [(i, i ^ offset) for i in range(total)])  30.3 us
    ppermute x27, waiting for transfers between devices, xor_permute(): return lax.ppermute(value, AXES, [(i, i ^ offset) for i in range(total)])  23.8 us
    all_to_all x1, waiting for transfers between devices, on_device_small(): sums = lax.all_to_all(sums, AXES, split_axis=0, concat_axis=0)  7.59 us
    all_to_all x1, starting transfers between devices, on_device_small(): sums = lax.all_to_all(sums, AXES, split_axis=0, concat_axis=0)  3.35 us
    pallas_call x1, Pallas kernels, attention(): local_call(functools.partial(attention_kernel, pieces=len(pieces), heads=...  2.73 us
    pallas_call x1, Pallas kernels, pack(): local_call(functools.partial(pack_kernel, block=block), 'pack', [jax.Shap...  2.28 us
    pallas_call x5, Pallas kernels, kv_terms(): local_call(functools.partial(terms_kernel, groups=groups, rows=rows), 'kv...  1.85 us
  transfers between devices with their start and end apart: 28, of which 12 were waited for; matrix products, arithmetic and copies ran while one was open for 1% of the time, Pallas kernels for 10%

profile of v2, /device:TPU:0, one launch (start us, length us, event | category | flops | bytes accessed | tf_op | source)
XLA Modules:
  0.0 79.2 jit_solution(11140340949582545857)
XLA Ops:
  0.7 2.3 %pack.1 = (bf16[144,256]{1,0:T(8,128)(2,1)}, bf16[128,4096]{1,0:T(8,128)(2,1)}) custom-call(bf16[128,128]{1,0:T(8,128)(2,1)} %bitcast.17, bf16[128,128]{1,0:T(8,128)(2,1)} %bitcast.19, s32[1,128]{1,0:T(1,128)} %ids_ref.3, bf16[128,8192]{1,0:T(8,128)(2,1)} %bitcast.9), custom_call_target="tpu_custom_call" | custom-call | bytes 2097152 | tf_op jit(solution)/shard_map/pack/pallas_call | solution.py:111
  3.0 3.0 %collective-permute-start.14 = (bf16[128,4096]{1,0:T(8,128)(2,1)}, bf16[128,4096]{1,0:T(8,128)(2,1)S(1)}, u32[]{:S(2)}, u32[]{:S(2)}) collective-permute-start(bf16[128,4096]{1,0:T(8,128)(2,1)} %get-tuple-element.60), channel_id=1, source_target_pairs={{0,2},{1,3},{2,0},{3,1},{4,6},{5,7},{6,4},{7,5},{8,10},{9,11},{10,... | collective-permute-start | bytes 3145736 | tf_op jit(solution)/shard_map/ppermute | solution.py:31
  6.0 1.6 %collective-permute-start.1 = (bf16[144,256]{1,0:T(8,128)(2,1)}, bf16[144,256]{1,0:T(8,128)(2,1)S(1)}, u32[]{:S(2)}, u32[]{:S(2)}) collective-permute-start(bf16[144,256]{1,0:T(8,128)(2,1)} %get-tuple-element.51), channel_id=1, source_target_pairs={{0,8},{1,9},{2,10},{3,11},{4,12},{5,13},{6,14},{7,15},{8,0},{9,1},... | collective-permute-start | bytes 221192 | tf_op jit(solution)/shard_map/ppermute | solution.py:31
  7.6 2.6 %collective-permute-start.3 = (bf16[144,256]{1,0:T(8,128)(2,1)}, bf16[144,256]{1,0:T(8,128)(2,1)S(1)}, u32[]{:S(2)}, u32[]{:S(2)}) collective-permute-start(bf16[144,256]{1,0:T(8,128)(2,1)} %get-tuple-element.51), channel_id=1, source_target_pairs={{0,16},{1,17},{2,18},{3,19},{4,20},{5,21},{6,22},{7,23},{8,24},{9,... | collective-permute-start | bytes 221192 | tf_op jit(solution)/shard_map/ppermute | solution.py:31
  10.4 1.5 %collective-permute-start = (bf16[144,256]{1,0:T(8,128)(2,1)}, bf16[144,256]{1,0:T(8,128)(2,1)S(1)}, u32[]{:S(2)}, u32[]{:S(2)}) collective-permute-start(bf16[144,256]{1,0:T(8,128)(2,1)} %get-tuple-element.51), channel_id=1, source_target_pairs={{0,4},{1,5},{2,6},{3,7},{4,0},{5,1},{6,2},{7,3},{8,12},{9,13},{10,... | collective-permute-start | bytes 221192 | tf_op jit(solution)/shard_map/ppermute | solution.py:31
  12.4 2.9 %collective-permute-done.3.refs_4_ = bf16[144,256]{1,0:T(8,128)(2,1)S(1)} collective-permute-done((bf16[144,256]{1,0:T(8,128)(2,1)}, bf16[144,256]{1,0:T(8,128)(2,1)S(1)}, u32[]{:S(2)}, u32[]{:S(2)}) %collective-permute-start.3) | collective-permute-done | bytes 73760 | tf_op jit(solution)/shard_map/ppermute | solution.py:31
  15.3 1.5 %collective-permute-start.4 = (bf16[144,256]{1,0:T(8,128)(2,1)S(1)}, bf16[144,256]{1,0:T(8,128)(2,1)S(1)}, u32[]{:S(2)}, u32[]{:S(2)}) collective-permute-start(bf16[144,256]{1,0:T(8,128)(2,1)S(1)} %collective-permute-done.3.refs_4_), channel_id=1, source_target_pairs={{0,4},{1,5},{2,6},{3,7},{4,0},{5,1},{6,2},{7,3},{8,12},{9,13},{10,... | collective-permute-start | bytes 221192 | tf_op jit(solution)/shard_map/ppermute | solution.py:31
  16.8 1.3 %collective-permute-start.6 = (bf16[144,256]{1,0:T(8,128)(2,1)S(1)}, bf16[144,256]{1,0:T(8,128)(2,1)S(1)}, u32[]{:S(2)}, u32[]{:S(2)}) collective-permute-start(bf16[144,256]{1,0:T(8,128)(2,1)S(1)} %collective-permute-done.5.refs_6_), channel_id=1, source_target_pairs={{0,4},{1,5},{2,6},{3,7},{4,0},{5,1},{6,2},{7,3},{8,12},{9,13},{10,... | collective-permute-start | bytes 221192 | tf_op jit(solution)/shard_map/ppermute | solution.py:31
  19.7 1.5 %collective-permute-done.6.refs_7_ = bf16[144,256]{1,0:T(8,128)(2,1)S(1)} collective-permute-done((bf16[144,256]{1,0:T(8,128)(2,1)S(1)}, bf16[144,256]{1,0:T(8,128)(2,1)S(1)}, u32[]{:S(2)}, u32[]{:S(2)}) %collective-permute-start.6) | collective-permute-done | bytes 73760 | tf_op jit(solution)/shard_map/ppermute | solution.py:31
  21.2 2.7 %attention_scores.1 = (bf16[1024,1024]{1,0:T(8,128)(2,1)S(1)}, bf16[1024,1024]{1,0:T(8,128)(2,1)S(1)}, bf16[128,1024]{1,0:T(8,128)(2,1)S(1)}) custom-call(bf16[1024,128]{1,0:T(8,128)(2,1)S(1)} %get-tuple-element.46.q_all, bf16[1024,128]{1,0:T(8,128)(2,1)S(1)} %get-tuple-element.47.g_all, f32[1,1024]{1,0:T(1,128)S(1)} %get-tuple-element.48.delta_ref, ...), custom_call_target="tpu_custom_call" | custom-call | flops 536870912 | bytes 4194304 | tf_op jit(solution)/shard_map/attention_scores/pallas_call | solution.py:247
  24.2 1.4 %collective-permute-start.12 = (bf16[128,256]{1,0:T(8,128)(2,1)S(1)}, bf16[128,256]{1,0:T(8,128)(2,1)S(1)}, u32[]{:S(2)}, u32[]{:S(2)}) collective-permute-start(bf16[128,256]{1,0:T(8,128)(2,1)S(1)} %kv_terms.5.refs_0_), channel_id=1, source_target_pairs={{0,4},{1,5},{2,6},{3,7},{4,0},{5,1},{6,2},{7,3},{8,12},{9,13},{10,... | collective-permute-start | bytes 196616 | tf_op jit(solution)/shard_map/ppermute | solution.py:31
  27.0 1.4 %collective-permute-start.8 = (bf16[128,256]{1,0:T(8,128)(2,1)S(1)}, bf16[128,256]{1,0:T(8,128)(2,1)S(1)}, u32[]{:S(2)}, u32[]{:S(2)}) collective-permute-start(bf16[128,256]{1,0:T(8,128)(2,1)S(1)} %kv_terms.7.refs_0_), channel_id=1, source_target_pairs={{0,4},{1,5},{2,6},{3,7},{4,0},{5,1},{6,2},{7,3},{8,12},{9,13},{10,... | collective-permute-start | bytes 196616 | tf_op jit(solution)/shard_map/ppermute | solution.py:31
  30.1 3.3 %collective-permute-start.13 = (bf16[128,256]{1,0:T(8,128)(2,1)S(1)}, bf16[128,256]{1,0:T(8,128)(2,1)S(1)}, u32[]{:S(2)}, u32[]{:S(2)}) collective-permute-start(bf16[128,256]{1,0:T(8,128)(2,1)S(1)} %combine.15), channel_id=1, source_target_pairs={{0,24},{1,25},{2,26},{3,27},{4,28},{5,29},{6,30},{7,31},{8,16},{9,... | collective-permute-start | bytes 196616 | tf_op jit(solution)/shard_map/ppermute | solution.py:31
  34.8 1.2 %query_gradient.1 = (bf16[128,1024]{1,0:T(8,128)(2,1)}, f32[8,128]{1,0:T(8,128)S(1)}) custom-call(bf16[128,1024]{1,0:T(8,128)(2,1)S(1)} %get-tuple-element.52.k_t, bf16[1024,1024]{1,0:T(8,128)(2,1)S(1)} %get-tuple-element.53.grads_t), custom_call_target="tpu_custom_call" | custom-call | flops 268435456 | bytes 2097152 | tf_op jit(solution)/shard_map/query_gradient/pallas_call | solution.py:306
  36.3 2.4 %collective-permute-done.11.refs_2_ = bf16[128,256]{1,0:T(8,128)(2,1)S(1)} collective-permute-done((bf16[128,256]{1,0:T(8,128)(2,1)S(1)}, bf16[128,256]{1,0:T(8,128)(2,1)S(1)}, u32[]{:S(2)}, u32[]{:S(2)}) %collective-permute-start.11) | collective-permute-done | bytes 65568 | tf_op jit(solution)/shard_map/ppermute | solution.py:31
  39.3 3.8 %collective-permute-done.15.other_kv = bf16[128,256]{1,0:T(8,128)(2,1)S(1)} collective-permute-done((bf16[128,256]{1,0:T(8,128)(2,1)S(1)}, bf16[128,256]{1,0:T(8,128)(2,1)S(1)}, u32[]{:S(2)}, u32[]{:S(2)}) %collective-permute-start.15) | collective-permute-done | bytes 65568 | tf_op jit(solution)/shard_map/ppermute | solution.py:31
  46.7 1.3 %collective-permute-start.24 = (bf16[256,256]{1,0:T(8,128)(2,1)S(1)}, bf16[256,256]{1,0:T(8,128)(2,1)S(1)}, u32[]{:S(2)}, u32[]{:S(2)}) collective-permute-start(bf16[256,256]{1,0:T(8,128)(2,1)S(1)} %get-tuple-element.73.refs_0_), channel_id=1, source_target_pairs={{0,4},{1,5},{2,6},{3,7},{4,0},{5,1},{6,2},{7,3},{8,12},{9,13},{10,... | collective-permute-start | bytes 393224 | tf_op jit(solution)/shard_map/ppermute | solution.py:31
  48.0 4.2 %collective-permute-done.20.other_ref = bf16[256,256]{1,0:T(8,128)(2,1)S(1)} collective-permute-done((bf16[256,256]{1,0:T(8,128)(2,1)S(1)}, bf16[256,256]{1,0:T(8,128)(2,1)S(1)}, u32[]{:S(2)}, u32[]{:S(2)}) %collective-permute-start.20) | collective-permute-done | bytes 131104 | tf_op jit(solution)/shard_map/ppermute | solution.py:31
  53.1 2.2 %collective-permute-start.26 = (bf16[256,256]{1,0:T(8,128)(2,1)S(1)}, bf16[256,256]{1,0:T(8,128)(2,1)S(1)}, u32[]{:S(2)}, u32[]{:S(2)}) collective-permute-start(bf16[256,256]{1,0:T(8,128)(2,1)S(1)} %combine.18.refs_1_), channel_id=1, source_target_pairs={{0,24},{1,25},{2,26},{3,27},{4,28},{5,29},{6,30},{7,31},{8,16},{9,... | collective-permute-start | bytes 393224 | tf_op jit(solution)/shard_map/ppermute | solution.py:31
  57.1 1.5 %collective-permute-done.22.other_ref = bf16[256,256]{1,0:T(8,128)(2,1)S(1)} collective-permute-done((bf16[256,256]{1,0:T(8,128)(2,1)S(1)}, bf16[256,256]{1,0:T(8,128)(2,1)S(1)}, u32[]{:S(2)}, u32[]{:S(2)}) %collective-permute-start.22) | collective-permute-done | bytes 131104 | tf_op jit(solution)/shard_map/ppermute | solution.py:31
  59.1 1.3 %collective-permute-done.21.other_ref = bf16[256,256]{1,0:T(8,128)(2,1)S(1)} collective-permute-done((bf16[256,256]{1,0:T(8,128)(2,1)S(1)}, bf16[256,256]{1,0:T(8,128)(2,1)S(1)}, u32[]{:S(2)}, u32[]{:S(2)}) %collective-permute-start.21) | collective-permute-done | bytes 131104 | tf_op jit(solution)/shard_map/ppermute | solution.py:31
  60.5 5.1 %collective-permute-done.25.refs_2_ = bf16[256,256]{1,0:T(8,128)(2,1)S(1)} collective-permute-done((bf16[256,256]{1,0:T(8,128)(2,1)S(1)}, bf16[256,256]{1,0:T(8,128)(2,1)S(1)}, u32[]{:S(2)}, u32[]{:S(2)}) %collective-permute-start.25) | collective-permute-done | bytes 131104 | tf_op jit(solution)/shard_map/ppermute | solution.py:31
  66.7 3.3 %all-to-all-start = ((f32[32,8,128]{2,1,0:T(8,128)}), f32[32,8,128]{2,1,0:T(8,128)S(1)}, u32[]{:S(2)}, u32[]{:S(2)}) async-start(f32[32,8,128]{2,1,0:T(8,128)} %get-tuple-element.80), calls=%async_computation | async-start | bytes 262144 | tf_op jit(solution)/shard_map/all_to_all | solution.py:532
  70.7 7.6 %all-to-all-done.sums_ref = f32[32,8,128]{2,1,0:T(8,128)S(1)} async-done(((f32[32,8,128]{2,1,0:T(8,128)}), f32[32,8,128]{2,1,0:T(8,128)S(1)}, u32[]{:S(2)}, u32[]{:S(2)}) %all-to-all-start) | async-done | bytes 131104 | tf_op jit(solution)/shard_map/all_to_all | solution.py:532
  (83 shorter events, 17.2 us)
Async XLA Ops:
  3.0 35.7 %collective-permute-start.14 = (bf16[128,4096]{1,0:T(8,128)(2,1)}, bf16[128,4096]{1,0:T(8,128)(2,1)S(1)}, u32[]{:S(2)}, u32[]{:S(2)}) collective-permute-start(bf16[128,4096]{1,0:T(8,128)(2,1)} %get-tuple-element.60), channel_id=1, source_target_pairs={{0,2},{1,3},{2,0},{3,1},{4,6},{5,7},{6,4},{7,5},{8,10},{9,11},{10,... | collective-permute-start | bytes 3145736 | tf_op jit(solution)/shard_map/ppermute | solution.py:31
  6.0 5.9 %collective-permute-start.1 = (bf16[144,256]{1,0:T(8,128)(2,1)}, bf16[144,256]{1,0:T(8,128)(2,1)S(1)}, u32[]{:S(2)}, u32[]{:S(2)}) collective-permute-start(bf16[144,256]{1,0:T(8,128)(2,1)} %get-tuple-element.51), channel_id=1, source_target_pairs={{0,8},{1,9},{2,10},{3,11},{4,12},{5,13},{6,14},{7,15},{8,0},{9,1},... | collective-permute-start | bytes 221192 | tf_op jit(solution)/shard_map/ppermute | solution.py:31
  7.6 7.7 %collective-permute-start.3 = (bf16[144,256]{1,0:T(8,128)(2,1)}, bf16[144,256]{1,0:T(8,128)(2,1)S(1)}, u32[]{:S(2)}, u32[]{:S(2)}) collective-permute-start(bf16[144,256]{1,0:T(8,128)(2,1)} %get-tuple-element.51), channel_id=1, source_target_pairs={{0,16},{1,17},{2,18},{3,19},{4,20},{5,21},{6,22},{7,23},{8,24},{9,... | collective-permute-start | bytes 221192 | tf_op jit(solution)/shard_map/ppermute | solution.py:31
  10.2 6.6 %collective-permute-start.5 = (bf16[144,256]{1,0:T(8,128)(2,1)}, bf16[144,256]{1,0:T(8,128)(2,1)S(1)}, u32[]{:S(2)}, u32[]{:S(2)}) collective-permute-start(bf16[144,256]{1,0:T(8,128)(2,1)} %get-tuple-element.51), channel_id=1, source_target_pairs={{0,24},{1,25},{2,26},{3,27},{4,28},{5,29},{6,30},{7,31},{8,16},{9,... | collective-permute-start | bytes 221192 | tf_op jit(solution)/shard_map/ppermute | solution.py:31
  10.4 8.6 %collective-permute-start = (bf16[144,256]{1,0:T(8,128)(2,1)}, bf16[144,256]{1,0:T(8,128)(2,1)S(1)}, u32[]{:S(2)}, u32[]{:S(2)}) collective-permute-start(bf16[144,256]{1,0:T(8,128)(2,1)} %get-tuple-element.51), channel_id=1, source_target_pairs={{0,4},{1,5},{2,6},{3,7},{4,0},{5,1},{6,2},{7,3},{8,12},{9,13},{10,... | collective-permute-start | bytes 221192 | tf_op jit(solution)/shard_map/ppermute | solution.py:31
  11.9 7.1 %collective-permute-start.2 = (bf16[144,256]{1,0:T(8,128)(2,1)S(1)}, bf16[144,256]{1,0:T(8,128)(2,1)S(1)}, u32[]{:S(2)}, u32[]{:S(2)}) collective-permute-start(bf16[144,256]{1,0:T(8,128)(2,1)S(1)} %collective-permute-done.1.refs_2_), channel_id=1, source_target_pairs={{0,4},{1,5},{2,6},{3,7},{4,0},{5,1},{6,2},{7,3},{8,12},{9,13},{10,... | collective-permute-start | bytes 221192 | tf_op jit(solution)/shard_map/ppermute | solution.py:31
  16.8 4.4 %collective-permute-start.6 = (bf16[144,256]{1,0:T(8,128)(2,1)S(1)}, bf16[144,256]{1,0:T(8,128)(2,1)S(1)}, u32[]{:S(2)}, u32[]{:S(2)}) collective-permute-start(bf16[144,256]{1,0:T(8,128)(2,1)S(1)} %collective-permute-done.5.refs_6_), channel_id=1, source_target_pairs={{0,4},{1,5},{2,6},{3,7},{4,0},{5,1},{6,2},{7,3},{8,12},{9,13},{10,... | collective-permute-start | bytes 221192 | tf_op jit(solution)/shard_map/ppermute | solution.py:31
  24.2 5.9 %collective-permute-start.12 = (bf16[128,256]{1,0:T(8,128)(2,1)S(1)}, bf16[128,256]{1,0:T(8,128)(2,1)S(1)}, u32[]{:S(2)}, u32[]{:S(2)}) collective-permute-start(bf16[128,256]{1,0:T(8,128)(2,1)S(1)} %kv_terms.5.refs_0_), channel_id=1, source_target_pairs={{0,4},{1,5},{2,6},{3,7},{4,0},{5,1},{6,2},{7,3},{8,12},{9,13},{10,... | collective-permute-start | bytes 196616 | tf_op jit(solution)/shard_map/ppermute | solution.py:31
  25.9 7.6 %collective-permute-start.10 = (bf16[128,256]{1,0:T(8,128)(2,1)S(1)}, bf16[128,256]{1,0:T(8,128)(2,1)S(1)}, u32[]{:S(2)}, u32[]{:S(2)}) collective-permute-start(bf16[128,256]{1,0:T(8,128)(2,1)S(1)} %kv_terms.6.refs_0_), channel_id=1, source_target_pairs={{0,4},{1,5},{2,6},{3,7},{4,0},{5,1},{6,2},{7,3},{8,12},{9,13},{10,... | collective-permute-start | bytes 196616 | tf_op jit(solution)/shard_map/ppermute | solution.py:31
  27.0 6.6 %collective-permute-start.8 = (bf16[128,256]{1,0:T(8,128)(2,1)S(1)}, bf16[128,256]{1,0:T(8,128)(2,1)S(1)}, u32[]{:S(2)}, u32[]{:S(2)}) collective-permute-start(bf16[128,256]{1,0:T(8,128)(2,1)S(1)} %kv_terms.7.refs_0_), channel_id=1, source_target_pairs={{0,4},{1,5},{2,6},{3,7},{4,0},{5,1},{6,2},{7,3},{8,12},{9,13},{10,... | collective-permute-start | bytes 196616 | tf_op jit(solution)/shard_map/ppermute | solution.py:31
  28.6 7.4 %collective-permute-start.7 = (bf16[128,256]{1,0:T(8,128)(2,1)S(1)}, bf16[128,256]{1,0:T(8,128)(2,1)S(1)}, u32[]{:S(2)}, u32[]{:S(2)}) collective-permute-start(bf16[128,256]{1,0:T(8,128)(2,1)S(1)} %kv_terms.8.refs_0_), channel_id=1, source_target_pairs={{0,4},{1,5},{2,6},{3,7},{4,0},{5,1},{6,2},{7,3},{8,12},{9,13},{10,... | collective-permute-start | bytes 196616 | tf_op jit(solution)/shard_map/ppermute | solution.py:31
  30.1 6.1 %collective-permute-start.13 = (bf16[128,256]{1,0:T(8,128)(2,1)S(1)}, bf16[128,256]{1,0:T(8,128)(2,1)S(1)}, u32[]{:S(2)}, u32[]{:S(2)}) collective-permute-start(bf16[128,256]{1,0:T(8,128)(2,1)S(1)} %combine.15), channel_id=1, source_target_pairs={{0,24},{1,25},{2,26},{3,27},{4,28},{5,29},{6,30},{7,31},{8,16},{9,... | collective-permute-start | bytes 196616 | tf_op jit(solution)/shard_map/ppermute | solution.py:31
  33.5 5.2 %collective-permute-start.11 = (bf16[128,256]{1,0:T(8,128)(2,1)S(1)}, bf16[128,256]{1,0:T(8,128)(2,1)S(1)}, u32[]{:S(2)}, u32[]{:S(2)}) collective-permute-start(bf16[128,256]{1,0:T(8,128)(2,1)S(1)} %combine.14), channel_id=1, source_target_pairs={{0,16},{1,17},{2,18},{3,19},{4,20},{5,21},{6,22},{7,23},{8,24},{9,... | collective-permute-start | bytes 196616 | tf_op jit(solution)/shard_map/ppermute | solution.py:31
  33.6 5.1 %collective-permute-start.9 = (bf16[128,256]{1,0:T(8,128)(2,1)S(1)}, bf16[128,256]{1,0:T(8,128)(2,1)S(1)}, u32[]{:S(2)}, u32[]{:S(2)}) collective-permute-start(bf16[128,256]{1,0:T(8,128)(2,1)S(1)} %combine.13), channel_id=1, source_target_pairs={{0,8},{1,9},{2,10},{3,11},{4,12},{5,13},{6,14},{7,15},{8,0},{9,1},... | collective-permute-start | bytes 196616 | tf_op jit(solution)/shard_map/ppermute | solution.py:31
  44.7 7.5 %collective-permute-start.17 = (bf16[256,512]{1,0:T(8,128)(2,1)S(1)}, bf16[256,512]{1,0:T(8,128)(2,1)S(1)}, u32[]{:S(2)}, u32[]{:S(2)}) collective-permute-start(bf16[256,512]{1,0:T(8,128)(2,1)S(1)} %get-tuple-element.67), channel_id=1, source_target_pairs={{0,1},{1,0},{2,3},{3,2},{4,5},{5,4},{6,7},{7,6},{8,9},{9,8},{10,11... | collective-permute-start | bytes 786440 | tf_op jit(solution)/shard_map/ppermute | solution.py:31
  45.1 10.2 %collective-permute-start.16 = (bf16[256,512]{1,0:T(8,128)(2,1)S(1)}, bf16[256,512]{1,0:T(8,128)(2,1)S(1)}, u32[]{:S(2)}, u32[]{:S(2)}) collective-permute-start(bf16[256,512]{1,0:T(8,128)(2,1)S(1)} %get-tuple-element.65), channel_id=1, source_target_pairs={{0,1},{1,0},{2,3},{3,2},{4,5},{5,4},{6,7},{7,6},{8,9},{9,8},{10,11... | collective-permute-start | bytes 786440 | tf_op jit(solution)/shard_map/ppermute | solution.py:31
  45.8 6.4 %collective-permute-start.20 = (bf16[256,256]{1,0:T(8,128)(2,1)S(1)}, bf16[256,256]{1,0:T(8,128)(2,1)S(1)}, u32[]{:S(2)}, u32[]{:S(2)}) collective-permute-start(bf16[256,256]{1,0:T(8,128)(2,1)S(1)} %get-tuple-element.72.refs_0_), channel_id=1, source_target_pairs={{0,4},{1,5},{2,6},{3,7},{4,0},{5,1},{6,2},{7,3},{8,12},{9,13},{10,... | collective-permute-start | bytes 393224 | tf_op jit(solution)/shard_map/ppermute | solution.py:31
  46.7 9.8 %collective-permute-start.24 = (bf16[256,256]{1,0:T(8,128)(2,1)S(1)}, bf16[256,256]{1,0:T(8,128)(2,1)S(1)}, u32[]{:S(2)}, u32[]{:S(2)}) collective-permute-start(bf16[256,256]{1,0:T(8,128)(2,1)S(1)} %get-tuple-element.73.refs_0_), channel_id=1, source_target_pairs={{0,4},{1,5},{2,6},{3,7},{4,0},{5,1},{6,2},{7,3},{8,12},{9,13},{10,... | collective-permute-start | bytes 393224 | tf_op jit(solution)/shard_map/ppermute | solution.py:31
  52.3 6.3 %collective-permute-start.22 = (bf16[256,256]{1,0:T(8,128)(2,1)S(1)}, bf16[256,256]{1,0:T(8,128)(2,1)S(1)}, u32[]{:S(2)}, u32[]{:S(2)}) collective-permute-start(bf16[256,256]{1,0:T(8,128)(2,1)S(1)} %get-tuple-element.75.refs_0_), channel_id=1, source_target_pairs={{0,4},{1,5},{2,6},{3,7},{4,0},{5,1},{6,2},{7,3},{8,12},{9,13},{10,... | collective-permute-start | bytes 393224 | tf_op jit(solution)/shard_map/ppermute | solution.py:31
  53.1 12.4 %collective-permute-start.26 = (bf16[256,256]{1,0:T(8,128)(2,1)S(1)}, bf16[256,256]{1,0:T(8,128)(2,1)S(1)}, u32[]{:S(2)}, u32[]{:S(2)}) collective-permute-start(bf16[256,256]{1,0:T(8,128)(2,1)S(1)} %combine.18.refs_1_), channel_id=1, source_target_pairs={{0,24},{1,25},{2,26},{3,27},{4,28},{5,29},{6,30},{7,31},{8,16},{9,... | collective-permute-start | bytes 393224 | tf_op jit(solution)/shard_map/ppermute | solution.py:31
  55.4 5.0 %collective-permute-start.21 = (bf16[256,256]{1,0:T(8,128)(2,1)S(1)}, bf16[256,256]{1,0:T(8,128)(2,1)S(1)}, u32[]{:S(2)}, u32[]{:S(2)}) collective-permute-start(bf16[256,256]{1,0:T(8,128)(2,1)S(1)} %get-tuple-element.77), channel_id=1, source_target_pairs={{0,4},{1,5},{2,6},{3,7},{4,0},{5,1},{6,2},{7,3},{8,12},{9,13},{10,... | collective-permute-start | bytes 393224 | tf_op jit(solution)/shard_map/ppermute | solution.py:31
  56.5 9.0 %collective-permute-start.25 = (bf16[256,256]{1,0:T(8,128)(2,1)S(1)}, bf16[256,256]{1,0:T(8,128)(2,1)S(1)}, u32[]{:S(2)}, u32[]{:S(2)}) collective-permute-start(bf16[256,256]{1,0:T(8,128)(2,1)S(1)} %combine.23), channel_id=1, source_target_pairs={{0,16},{1,17},{2,18},{3,19},{4,20},{5,21},{6,22},{7,23},{8,24},{9,... | collective-permute-start | bytes 393224 | tf_op jit(solution)/shard_map/ppermute | solution.py:31
  58.6 7.1 %collective-permute-start.23 = (bf16[256,256]{1,0:T(8,128)(2,1)S(1)}, bf16[256,256]{1,0:T(8,128)(2,1)S(1)}, u32[]{:S(2)}, u32[]{:S(2)}) collective-permute-start(bf16[256,256]{1,0:T(8,128)(2,1)S(1)} %combine.22), channel_id=1, source_target_pairs={{0,8},{1,9},{2,10},{3,11},{4,12},{5,13},{6,14},{7,15},{8,0},{9,1},... | collective-permute-start | bytes 393224 | tf_op jit(solution)/shard_map/ppermute | solution.py:31
  66.7 11.6 %all-to-all-start = ((f32[32,8,128]{2,1,0:T(8,128)}), f32[32,8,128]{2,1,0:T(8,128)S(1)}, u32[]{:S(2)}, u32[]{:S(2)}) async-start(f32[32,8,128]{2,1,0:T(8,128)} %get-tuple-element.80), calls=%async_computation | async-start | bytes 262144 | tf_op jit(solution)/shard_map/all_to_all | solution.py:532
  (15 other events, 186.1 us)

commit v3 on v2

--- a/solution.py
+++ b/solution.py
@@ -520,7 +520,8 @@
     blocks, after = {}, []
     for group in chunk_groups(planes):
         step = group[0][2]
-        keep, send = project(activations[0], other_acts, kvs, [], group, block)
+        ahead = [blocks[planes - 1]] if step < planes // 2 else []
+        keep, send = project(activations[0], other_acts, kvs, ahead, group, block)
         keep, send = combine(keep, xor_permute(send, core, total), [full, low], 1, after)
         after = [send]
         if step == planes // 2:

time: 79.4 us -> 81.7 us (1.029)
  waiting for transfers between devices: 31.4 us -> 33.2 us
    ppermute x27, waiting for transfers between devices: 23.8 us -> 25.7 us  [xor_permute(): return lax.ppermute(value, AXES, [(i, i ^ offset) for i in range(total)])]
  transfers between devices with their start and end apart: 28 -> 28, of which waited for: 12 -> 13; matrix products, arithmetic and copies ran while one was open for 1% -> 1% of each run, Pallas kernels for 10% -> 10%
where the time goes in v3:
time: 81.7 us; the launch traced here: 81.5 us
  starting transfers between devices  34.1 us (42%)
  waiting for transfers between devices  33.2 us (41%)
  Pallas kernels  12.5 us (15%)
  between operations  0.98 us (1%)
    ppermute x27, starting transfers between devices, xor_permute(): return lax.ppermute(value, AXES, [(i, i ^ offset) for i in range(total)])  31.2 us
    ppermute x27, waiting for transfers between devices, xor_permute(): return lax.ppermute(value, AXES, [(i, i ^ offset) for i in range(total)])  25.7 us
    all_to_all x1, waiting for transfers between devices, on_device_small(): sums = lax.all_to_all(sums, AXES, split_axis=0, concat_axis=0)  7.59 us
    all_to_all x1, starting transfers between devices, on_device_small(): sums = lax.all_to_all(sums, AXES, split_axis=0, concat_axis=0)  2.94 us
    pallas_call x1, Pallas kernels, attention(): local_call(functools.partial(attention_kernel, pieces=len(pieces), heads=...  2.73 us
    pallas_call x1, Pallas kernels, pack(): local_call(functools.partial(pack_kernel, block=block), 'pack', [jax.Shap...  2.28 us
    pallas_call x5, Pallas kernels, kv_terms(): local_call(functools.partial(terms_kernel, groups=groups, rows=rows), 'kv...  1.85 us
  transfers between devices with their start and end apart: 28, of which 13 were waited for; matrix products, arithmetic and copies ran while one was open for 1% of the time, Pallas kernels for 10%

profile of v3, /device:TPU:0, one launch (start us, length us, event | category | flops | bytes accessed | tf_op | source)
XLA Modules:
  0.0 81.5 jit_solution(15270163222476319092)
XLA Ops:
  0.7 2.3 %pack.1 = (bf16[144,256]{1,0:T(8,128)(2,1)}, bf16[128,4096]{1,0:T(8,128)(2,1)}) custom-call(bf16[128,128]{1,0:T(8,128)(2,1)} %bitcast.17, bf16[128,128]{1,0:T(8,128)(2,1)} %bitcast.19, s32[1,128]{1,0:T(1,128)} %ids_ref.3, bf16[128,8192]{1,0:T(8,128)(2,1)} %bitcast.9), custom_call_target="tpu_custom_call" | custom-call | bytes 2097152 | tf_op jit(solution)/shard_map/pack/pallas_call | solution.py:111
  3.0 3.0 %collective-permute-start.14 = (bf16[128,4096]{1,0:T(8,128)(2,1)}, bf16[128,4096]{1,0:T(8,128)(2,1)S(1)}, u32[]{:S(2)}, u32[]{:S(2)}) collective-permute-start(bf16[128,4096]{1,0:T(8,128)(2,1)} %get-tuple-element.60), channel_id=1, source_target_pairs={{0,2},{1,3},{2,0},{3,1},{4,6},{5,7},{6,4},{7,5},{8,10},{9,11},{10,... | collective-permute-start | bytes 3145736 | tf_op jit(solution)/shard_map/ppermute | solution.py:31
  6.0 1.6 %collective-permute-start.1 = (bf16[144,256]{1,0:T(8,128)(2,1)}, bf16[144,256]{1,0:T(8,128)(2,1)S(1)}, u32[]{:S(2)}, u32[]{:S(2)}) collective-permute-start(bf16[144,256]{1,0:T(8,128)(2,1)} %get-tuple-element.51), channel_id=1, source_target_pairs={{0,8},{1,9},{2,10},{3,11},{4,12},{5,13},{6,14},{7,15},{8,0},{9,1},... | collective-permute-start | bytes 221192 | tf_op jit(solution)/shard_map/ppermute | solution.py:31
  7.6 2.6 %collective-permute-start.3 = (bf16[144,256]{1,0:T(8,128)(2,1)}, bf16[144,256]{1,0:T(8,128)(2,1)S(1)}, u32[]{:S(2)}, u32[]{:S(2)}) collective-permute-start(bf16[144,256]{1,0:T(8,128)(2,1)} %get-tuple-element.51), channel_id=1, source_target_pairs={{0,16},{1,17},{2,18},{3,19},{4,20},{5,21},{6,22},{7,23},{8,24},{9,... | collective-permute-start | bytes 221192 | tf_op jit(solution)/shard_map/ppermute | solution.py:31
  10.4 1.5 %collective-permute-start = (bf16[144,256]{1,0:T(8,128)(2,1)}, bf16[144,256]{1,0:T(8,128)(2,1)S(1)}, u32[]{:S(2)}, u32[]{:S(2)}) collective-permute-start(bf16[144,256]{1,0:T(8,128)(2,1)} %get-tuple-element.51), channel_id=1, source_target_pairs={{0,4},{1,5},{2,6},{3,7},{4,0},{5,1},{6,2},{7,3},{8,12},{9,13},{10,... | collective-permute-start | bytes 221192 | tf_op jit(solution)/shard_map/ppermute | solution.py:31
  12.4 2.9 %collective-permute-done.3.refs_4_ = bf16[144,256]{1,0:T(8,128)(2,1)S(1)} collective-permute-done((bf16[144,256]{1,0:T(8,128)(2,1)}, bf16[144,256]{1,0:T(8,128)(2,1)S(1)}, u32[]{:S(2)}, u32[]{:S(2)}) %collective-permute-start.3) | collective-permute-done | bytes 73760 | tf_op jit(solution)/shard_map/ppermute | solution.py:31
  15.3 1.5 %collective-permute-start.4 = (bf16[144,256]{1,0:T(8,128)(2,1)S(1)}, bf16[144,256]{1,0:T(8,128)(2,1)S(1)}, u32[]{:S(2)}, u32[]{:S(2)}) collective-permute-start(bf16[144,256]{1,0:T(8,128)(2,1)S(1)} %collective-permute-done.3.refs_4_), channel_id=1, source_target_pairs={{0,4},{1,5},{2,6},{3,7},{4,0},{5,1},{6,2},{7,3},{8,12},{9,13},{10,... | collective-permute-start | bytes 221192 | tf_op jit(solution)/shard_map/ppermute | solution.py:31
  16.8 1.3 %collective-permute-start.6 = (bf16[144,256]{1,0:T(8,128)(2,1)S(1)}, bf16[144,256]{1,0:T(8,128)(2,1)S(1)}, u32[]{:S(2)}, u32[]{:S(2)}) collective-permute-start(bf16[144,256]{1,0:T(8,128)(2,1)S(1)} %collective-permute-done.5.refs_6_), channel_id=1, source_target_pairs={{0,4},{1,5},{2,6},{3,7},{4,0},{5,1},{6,2},{7,3},{8,12},{9,13},{10,... | collective-permute-start | bytes 221192 | tf_op jit(solution)/shard_map/ppermute | solution.py:31
  19.7 1.5 %collective-permute-done.6.refs_7_ = bf16[144,256]{1,0:T(8,128)(2,1)S(1)} collective-permute-done((bf16[144,256]{1,0:T(8,128)(2,1)S(1)}, bf16[144,256]{1,0:T(8,128)(2,1)S(1)}, u32[]{:S(2)}, u32[]{:S(2)}) %collective-permute-start.6) | collective-permute-done | bytes 73760 | tf_op jit(solution)/shard_map/ppermute | solution.py:31
  21.2 2.7 %attention_scores.1 = (bf16[1024,1024]{1,0:T(8,128)(2,1)S(1)}, bf16[1024,1024]{1,0:T(8,128)(2,1)S(1)}, bf16[128,1024]{1,0:T(8,128)(2,1)S(1)}) custom-call(bf16[1024,128]{1,0:T(8,128)(2,1)S(1)} %get-tuple-element.46.q_all, bf16[1024,128]{1,0:T(8,128)(2,1)S(1)} %get-tuple-element.47.g_all, f32[1,1024]{1,0:T(1,128)S(1)} %get-tuple-element.48.delta_ref, ...), custom_call_target="tpu_custom_call" | custom-call | flops 536870912 | bytes 4194304 | tf_op jit(solution)/shard_map/attention_scores/pallas_call | solution.py:247
  24.2 1.4 %collective-permute-start.12 = (bf16[128,256]{1,0:T(8,128)(2,1)S(1)}, bf16[128,256]{1,0:T(8,128)(2,1)S(1)}, u32[]{:S(2)}, u32[]{:S(2)}) collective-permute-start(bf16[128,256]{1,0:T(8,128)(2,1)S(1)} %kv_terms.5.refs_0_), channel_id=1, source_target_pairs={{0,4},{1,5},{2,6},{3,7},{4,0},{5,1},{6,2},{7,3},{8,12},{9,13},{10,... | collective-permute-start | bytes 196616 | tf_op jit(solution)/shard_map/ppermute | solution.py:31
  27.0 1.4 %collective-permute-start.8 = (bf16[128,256]{1,0:T(8,128)(2,1)S(1)}, bf16[128,256]{1,0:T(8,128)(2,1)S(1)}, u32[]{:S(2)}, u32[]{:S(2)}) collective-permute-start(bf16[128,256]{1,0:T(8,128)(2,1)S(1)} %kv_terms.7.refs_0_), channel_id=1, source_target_pairs={{0,4},{1,5},{2,6},{3,7},{4,0},{5,1},{6,2},{7,3},{8,12},{9,13},{10,... | collective-permute-start | bytes 196616 | tf_op jit(solution)/shard_map/ppermute | solution.py:31
  30.1 3.3 %collective-permute-start.13 = (bf16[128,256]{1,0:T(8,128)(2,1)S(1)}, bf16[128,256]{1,0:T(8,128)(2,1)S(1)}, u32[]{:S(2)}, u32[]{:S(2)}) collective-permute-start(bf16[128,256]{1,0:T(8,128)(2,1)S(1)} %combine.15), channel_id=1, source_target_pairs={{0,24},{1,25},{2,26},{3,27},{4,28},{5,29},{6,30},{7,31},{8,16},{9,... | collective-permute-start | bytes 196616 | tf_op jit(solution)/shard_map/ppermute | solution.py:31
  36.3 2.4 %collective-permute-done.11.refs_2_ = bf16[128,256]{1,0:T(8,128)(2,1)S(1)} collective-permute-done((bf16[128,256]{1,0:T(8,128)(2,1)S(1)}, bf16[128,256]{1,0:T(8,128)(2,1)S(1)}, u32[]{:S(2)}, u32[]{:S(2)}) %collective-permute-start.11) | collective-permute-done | bytes 65568 | tf_op jit(solution)/shard_map/ppermute | solution.py:31
  39.3 3.8 %collective-permute-done.15.other_kv = bf16[128,256]{1,0:T(8,128)(2,1)S(1)} collective-permute-done((bf16[128,256]{1,0:T(8,128)(2,1)S(1)}, bf16[128,256]{1,0:T(8,128)(2,1)S(1)}, u32[]{:S(2)}, u32[]{:S(2)}) %collective-permute-start.15) | collective-permute-done | bytes 65568 | tf_op jit(solution)/shard_map/ppermute | solution.py:31
  43.5 1.5 %collective-permute-done.16.other_ref = bf16[256,512]{1,0:T(8,128)(2,1)S(1)} collective-permute-done((bf16[256,512]{1,0:T(8,128)(2,1)S(1)}, bf16[256,512]{1,0:T(8,128)(2,1)S(1)}, u32[]{:S(2)}, u32[]{:S(2)}) %collective-permute-start.16) | collective-permute-done | bytes 262176 | tf_op jit(solution)/shard_map/ppermute | solution.py:31
  46.3 4.3 %collective-permute-done.17.other_ref = bf16[256,256]{1,0:T(8,128)(2,1)S(1)} collective-permute-done((bf16[256,256]{1,0:T(8,128)(2,1)S(1)}, bf16[256,256]{1,0:T(8,128)(2,1)S(1)}, u32[]{:S(2)}, u32[]{:S(2)}) %collective-permute-start.17) | collective-permute-done | bytes 131104 | tf_op jit(solution)/shard_map/ppermute | solution.py:31
  53.0 1.3 %collective-permute-start.22 = (bf16[256,256]{1,0:T(8,128)(2,1)S(1)}, bf16[256,256]{1,0:T(8,128)(2,1)S(1)}, u32[]{:S(2)}, u32[]{:S(2)}) collective-permute-start(bf16[256,256]{1,0:T(8,128)(2,1)S(1)} %get-tuple-element.75.refs_0_), channel_id=1, source_target_pairs={{0,4},{1,5},{2,6},{3,7},{4,0},{5,1},{6,2},{7,3},{8,12},{9,13},{10,... | collective-permute-start | bytes 393224 | tf_op jit(solution)/shard_map/ppermute | solution.py:31
  54.3 2.0 %collective-permute-start.26 = (bf16[256,256]{1,0:T(8,128)(2,1)S(1)}, bf16[256,256]{1,0:T(8,128)(2,1)S(1)}, u32[]{:S(2)}, u32[]{:S(2)}) collective-permute-start(bf16[256,256]{1,0:T(8,128)(2,1)S(1)} %combine.17.refs_0_.refs_1_), channel_id=1, source_target_pairs={{0,24},{1,25},{2,26},{3,27},{4,28},{5,29},{6,30},{7,31},{8,16},{9,... | collective-permute-start | bytes 393224 | tf_op jit(solution)/shard_map/ppermute | solution.py:31
  56.3 2.2 %collective-permute-done.24.other_ref = bf16[256,256]{1,0:T(8,128)(2,1)S(1)} collective-permute-done((bf16[256,256]{1,0:T(8,128)(2,1)S(1)}, bf16[256,256]{1,0:T(8,128)(2,1)S(1)}, u32[]{:S(2)}, u32[]{:S(2)}) %collective-permute-start.24) | collective-permute-done | bytes 131104 | tf_op jit(solution)/shard_map/ppermute | solution.py:31
  59.5 2.1 %collective-permute-start.25 = (bf16[256,256]{1,0:T(8,128)(2,1)S(1)}, bf16[256,256]{1,0:T(8,128)(2,1)S(1)}, u32[]{:S(2)}, u32[]{:S(2)}) collective-permute-start(bf16[256,256]{1,0:T(8,128)(2,1)S(1)} %combine.23), channel_id=1, source_target_pairs={{0,16},{1,17},{2,18},{3,19},{4,20},{5,21},{6,22},{7,23},{8,24},{9,... | collective-permute-start | bytes 393224 | tf_op jit(solution)/shard_map/ppermute | solution.py:31
  63.7 4.4 %collective-permute-done.25.refs_2_ = bf16[256,256]{1,0:T(8,128)(2,1)S(1)} collective-permute-done((bf16[256,256]{1,0:T(8,128)(2,1)S(1)}, bf16[256,256]{1,0:T(8,128)(2,1)S(1)}, u32[]{:S(2)}, u32[]{:S(2)}) %collective-permute-start.25) | collective-permute-done | bytes 131104 | tf_op jit(solution)/shard_map/ppermute | solution.py:31
  69.5 2.9 %all-to-all-start = ((f32[32,8,128]{2,1,0:T(8,128)}), f32[32,8,128]{2,1,0:T(8,128)S(1)}, u32[]{:S(2)}, u32[]{:S(2)}) async-start(f32[32,8,128]{2,1,0:T(8,128)} %get-tuple-element.80), calls=%async_computation | async-start | bytes 262144 | tf_op jit(solution)/shard_map/all_to_all | solution.py:533
  73.1 7.6 %all-to-all-done.sums_ref = f32[32,8,128]{2,1,0:T(8,128)S(1)} async-done(((f32[32,8,128]{2,1,0:T(8,128)}), f32[32,8,128]{2,1,0:T(8,128)S(1)}, u32[]{:S(2)}, u32[]{:S(2)}) %all-to-all-start) | async-done | bytes 131104 | tf_op jit(solution)/shard_map/all_to_all | solution.py:533
  (83 shorter events, 18.9 us)
Async XLA Ops:
  3.0 35.7 %collective-permute-start.14 = (bf16[128,4096]{1,0:T(8,128)(2,1)}, bf16[128,4096]{1,0:T(8,128)(2,1)S(1)}, u32[]{:S(2)}, u32[]{:S(2)}) collective-permute-start(bf16[128,4096]{1,0:T(8,128)(2,1)} %get-tuple-element.60), channel_id=1, source_target_pairs={{0,2},{1,3},{2,0},{3,1},{4,6},{5,7},{6,4},{7,5},{8,10},{9,11},{10,... | collective-permute-start | bytes 3145736 | tf_op jit(solution)/shard_map/ppermute | solution.py:31
  6.0 5.9 %collective-permute-start.1 = (bf16[144,256]{1,0:T(8,128)(2,1)}, bf16[144,256]{1,0:T(8,128)(2,1)S(1)}, u32[]{:S(2)}, u32[]{:S(2)}) collective-permute-start(bf16[144,256]{1,0:T(8,128)(2,1)} %get-tuple-element.51), channel_id=1, source_target_pairs={{0,8},{1,9},{2,10},{3,11},{4,12},{5,13},{6,14},{7,15},{8,0},{9,1},... | collective-permute-start | bytes 221192 | tf_op jit(solution)/shard_map/ppermute | solution.py:31
  7.6 7.7 %collective-permute-start.3 = (bf16[144,256]{1,0:T(8,128)(2,1)}, bf16[144,256]{1,0:T(8,128)(2,1)S(1)}, u32[]{:S(2)}, u32[]{:S(2)}) collective-permute-start(bf16[144,256]{1,0:T(8,128)(2,1)} %get-tuple-element.51), channel_id=1, source_target_pairs={{0,16},{1,17},{2,18},{3,19},{4,20},{5,21},{6,22},{7,23},{8,24},{9,... | collective-permute-start | bytes 221192 | tf_op jit(solution)/shard_map/ppermute | solution.py:31
  10.2 6.6 %collective-permute-start.5 = (bf16[144,256]{1,0:T(8,128)(2,1)}, bf16[144,256]{1,0:T(8,128)(2,1)S(1)}, u32[]{:S(2)}, u32[]{:S(2)}) collective-permute-start(bf16[144,256]{1,0:T(8,128)(2,1)} %get-tuple-element.51), channel_id=1, source_target_pairs={{0,24},{1,25},{2,26},{3,27},{4,28},{5,29},{6,30},{7,31},{8,16},{9,... | collective-permute-start | bytes 221192 | tf_op jit(solution)/shard_map/ppermute | solution.py:31
  10.4 8.6 %collective-permute-start = (bf16[144,256]{1,0:T(8,128)(2,1)}, bf16[144,256]{1,0:T(8,128)(2,1)S(1)}, u32[]{:S(2)}, u32[]{:S(2)}) collective-permute-start(bf16[144,256]{1,0:T(8,128)(2,1)} %get-tuple-element.51), channel_id=1, source_target_pairs={{0,4},{1,5},{2,6},{3,7},{4,0},{5,1},{6,2},{7,3},{8,12},{9,13},{10,... | collective-permute-start | bytes 221192 | tf_op jit(solution)/shard_map/ppermute | solution.py:31
  11.9 7.1 %collective-permute-start.2 = (bf16[144,256]{1,0:T(8,128)(2,1)S(1)}, bf16[144,256]{1,0:T(8,128)(2,1)S(1)}, u32[]{:S(2)}, u32[]{:S(2)}) collective-permute-start(bf16[144,256]{1,0:T(8,128)(2,1)S(1)} %collective-permute-done.1.refs_2_), channel_id=1, source_target_pairs={{0,4},{1,5},{2,6},{3,7},{4,0},{5,1},{6,2},{7,3},{8,12},{9,13},{10,... | collective-permute-start | bytes 221192 | tf_op jit(solution)/shard_map/ppermute | solution.py:31
  16.8 4.4 %collective-permute-start.6 = (bf16[144,256]{1,0:T(8,128)(2,1)S(1)}, bf16[144,256]{1,0:T(8,128)(2,1)S(1)}, u32[]{:S(2)}, u32[]{:S(2)}) collective-permute-start(bf16[144,256]{1,0:T(8,128)(2,1)S(1)} %collective-permute-done.5.refs_6_), channel_id=1, source_target_pairs={{0,4},{1,5},{2,6},{3,7},{4,0},{5,1},{6,2},{7,3},{8,12},{9,13},{10,... | collective-permute-start | bytes 221192 | tf_op jit(solution)/shard_map/ppermute | solution.py:31
  24.2 5.9 %collective-permute-start.12 = (bf16[128,256]{1,0:T(8,128)(2,1)S(1)}, bf16[128,256]{1,0:T(8,128)(2,1)S(1)}, u32[]{:S(2)}, u32[]{:S(2)}) collective-permute-start(bf16[128,256]{1,0:T(8,128)(2,1)S(1)} %kv_terms.5.refs_0_), channel_id=1, source_target_pairs={{0,4},{1,5},{2,6},{3,7},{4,0},{5,1},{6,2},{7,3},{8,12},{9,13},{10,... | collective-permute-start | bytes 196616 | tf_op jit(solution)/shard_map/ppermute | solution.py:31
  25.9 7.6 %collective-permute-start.10 = (bf16[128,256]{1,0:T(8,128)(2,1)S(1)}, bf16[128,256]{1,0:T(8,128)(2,1)S(1)}, u32[]{:S(2)}, u32[]{:S(2)}) collective-permute-start(bf16[128,256]{1,0:T(8,128)(2,1)S(1)} %kv_terms.6.refs_0_), channel_id=1, source_target_pairs={{0,4},{1,5},{2,6},{3,7},{4,0},{5,1},{6,2},{7,3},{8,12},{9,13},{10,... | collective-permute-start | bytes 196616 | tf_op jit(solution)/shard_map/ppermute | solution.py:31
  27.0 6.6 %collective-permute-start.8 = (bf16[128,256]{1,0:T(8,128)(2,1)S(1)}, bf16[128,256]{1,0:T(8,128)(2,1)S(1)}, u32[]{:S(2)}, u32[]{:S(2)}) collective-permute-start(bf16[128,256]{1,0:T(8,128)(2,1)S(1)} %kv_terms.7.refs_0_), channel_id=1, source_target_pairs={{0,4},{1,5},{2,6},{3,7},{4,0},{5,1},{6,2},{7,3},{8,12},{9,13},{10,... | collective-permute-start | bytes 196616 | tf_op jit(solution)/shard_map/ppermute | solution.py:31
  28.6 7.4 %collective-permute-start.7 = (bf16[128,256]{1,0:T(8,128)(2,1)S(1)}, bf16[128,256]{1,0:T(8,128)(2,1)S(1)}, u32[]{:S(2)}, u32[]{:S(2)}) collective-permute-start(bf16[128,256]{1,0:T(8,128)(2,1)S(1)} %kv_terms.8.refs_0_), channel_id=1, source_target_pairs={{0,4},{1,5},{2,6},{3,7},{4,0},{5,1},{6,2},{7,3},{8,12},{9,13},{10,... | collective-permute-start | bytes 196616 | tf_op jit(solution)/shard_map/ppermute | solution.py:31
  30.1 6.1 %collective-permute-start.13 = (bf16[128,256]{1,0:T(8,128)(2,1)S(1)}, bf16[128,256]{1,0:T(8,128)(2,1)S(1)}, u32[]{:S(2)}, u32[]{:S(2)}) collective-permute-start(bf16[128,256]{1,0:T(8,128)(2,1)S(1)} %combine.15), channel_id=1, source_target_pairs={{0,24},{1,25},{2,26},{3,27},{4,28},{5,29},{6,30},{7,31},{8,16},{9,... | collective-permute-start | bytes 196616 | tf_op jit(solution)/shard_map/ppermute | solution.py:31
  33.5 5.2 %collective-permute-start.11 = (bf16[128,256]{1,0:T(8,128)(2,1)S(1)}, bf16[128,256]{1,0:T(8,128)(2,1)S(1)}, u32[]{:S(2)}, u32[]{:S(2)}) collective-permute-start(bf16[128,256]{1,0:T(8,128)(2,1)S(1)} %combine.14), channel_id=1, source_target_pairs={{0,16},{1,17},{2,18},{3,19},{4,20},{5,21},{6,22},{7,23},{8,24},{9,... | collective-permute-start | bytes 196616 | tf_op jit(solution)/shard_map/ppermute | solution.py:31
  33.6 5.1 %collective-permute-start.9 = (bf16[128,256]{1,0:T(8,128)(2,1)S(1)}, bf16[128,256]{1,0:T(8,128)(2,1)S(1)}, u32[]{:S(2)}, u32[]{:S(2)}) collective-permute-start(bf16[128,256]{1,0:T(8,128)(2,1)S(1)} %combine.13), channel_id=1, source_target_pairs={{0,8},{1,9},{2,10},{3,11},{4,12},{5,13},{6,14},{7,15},{8,0},{9,1},... | collective-permute-start | bytes 196616 | tf_op jit(solution)/shard_map/ppermute | solution.py:31
  45.1 5.6 %collective-permute-start.17 = (bf16[256,256]{1,0:T(8,128)(2,1)S(1)}, bf16[256,256]{1,0:T(8,128)(2,1)S(1)}, u32[]{:S(2)}, u32[]{:S(2)}) collective-permute-start(bf16[256,256]{1,0:T(8,128)(2,1)S(1)} %get-tuple-element.67.refs_0_), channel_id=1, source_target_pairs={{0,4},{1,5},{2,6},{3,7},{4,0},{5,1},{6,2},{7,3},{8,12},{9,13},{10,... | collective-permute-start | bytes 393224 | tf_op jit(solution)/shard_map/ppermute | solution.py:31
  46.3 5.8 %collective-permute-start.20 = (bf16[256,512]{1,0:T(8,128)(2,1)S(1)}, bf16[256,512]{1,0:T(8,128)(2,1)S(1)}, u32[]{:S(2)}, u32[]{:S(2)}) collective-permute-start(bf16[256,512]{1,0:T(8,128)(2,1)S(1)} %get-tuple-element.73), channel_id=1, source_target_pairs={{0,1},{1,0},{2,3},{3,2},{4,5},{5,4},{6,7},{7,6},{8,9},{9,8},{10,11... | collective-permute-start | bytes 786440 | tf_op jit(solution)/shard_map/ppermute | solution.py:31
  51.5 7.1 %collective-permute-start.18 = (bf16[256,512]{1,0:T(8,128)(2,1)S(1)}, bf16[256,512]{1,0:T(8,128)(2,1)S(1)}, u32[]{:S(2)}, u32[]{:S(2)}) collective-permute-start(bf16[256,512]{1,0:T(8,128)(2,1)S(1)} %get-tuple-element.69), channel_id=1, source_target_pairs={{0,1},{1,0},{2,3},{3,2},{4,5},{5,4},{6,7},{7,6},{8,9},{9,8},{10,11... | collective-permute-start | bytes 786440 | tf_op jit(solution)/shard_map/ppermute | solution.py:31
  52.1 6.4 %collective-permute-start.24 = (bf16[256,256]{1,0:T(8,128)(2,1)S(1)}, bf16[256,256]{1,0:T(8,128)(2,1)S(1)}, u32[]{:S(2)}, u32[]{:S(2)}) collective-permute-start(bf16[256,256]{1,0:T(8,128)(2,1)S(1)} %get-tuple-element.74.refs_0_), channel_id=1, source_target_pairs={{0,4},{1,5},{2,6},{3,7},{4,0},{5,1},{6,2},{7,3},{8,12},{9,13},{10,... | collective-permute-start | bytes 393224 | tf_op jit(solution)/shard_map/ppermute | solution.py:31
  53.0 8.6 %collective-permute-start.22 = (bf16[256,256]{1,0:T(8,128)(2,1)S(1)}, bf16[256,256]{1,0:T(8,128)(2,1)S(1)}, u32[]{:S(2)}, u32[]{:S(2)}) collective-permute-start(bf16[256,256]{1,0:T(8,128)(2,1)S(1)} %get-tuple-element.75.refs_0_), channel_id=1, source_target_pairs={{0,4},{1,5},{2,6},{3,7},{4,0},{5,1},{6,2},{7,3},{8,12},{9,13},{10,... | collective-permute-start | bytes 393224 | tf_op jit(solution)/shard_map/ppermute | solution.py:31
  54.3 13.8 %collective-permute-start.26 = (bf16[256,256]{1,0:T(8,128)(2,1)S(1)}, bf16[256,256]{1,0:T(8,128)(2,1)S(1)}, u32[]{:S(2)}, u32[]{:S(2)}) collective-permute-start(bf16[256,256]{1,0:T(8,128)(2,1)S(1)} %combine.17.refs_0_.refs_1_), channel_id=1, source_target_pairs={{0,24},{1,25},{2,26},{3,27},{4,28},{5,29},{6,30},{7,31},{8,16},{9,... | collective-permute-start | bytes 393224 | tf_op jit(solution)/shard_map/ppermute | solution.py:31
  58.6 5.0 %collective-permute-start.21 = (bf16[256,256]{1,0:T(8,128)(2,1)S(1)}, bf16[256,256]{1,0:T(8,128)(2,1)S(1)}, u32[]{:S(2)}, u32[]{:S(2)}) collective-permute-start(bf16[256,256]{1,0:T(8,128)(2,1)S(1)} %get-tuple-element.77), channel_id=1, source_target_pairs={{0,4},{1,5},{2,6},{3,7},{4,0},{5,1},{6,2},{7,3},{8,12},{9,13},{10,... | collective-permute-start | bytes 393224 | tf_op jit(solution)/shard_map/ppermute | solution.py:31
  59.5 8.6 %collective-permute-start.25 = (bf16[256,256]{1,0:T(8,128)(2,1)S(1)}, bf16[256,256]{1,0:T(8,128)(2,1)S(1)}, u32[]{:S(2)}, u32[]{:S(2)}) collective-permute-start(bf16[256,256]{1,0:T(8,128)(2,1)S(1)} %combine.23), channel_id=1, source_target_pairs={{0,16},{1,17},{2,18},{3,19},{4,20},{5,21},{6,22},{7,23},{8,24},{9,... | collective-permute-start | bytes 393224 | tf_op jit(solution)/shard_map/ppermute | solution.py:31
  61.6 6.8 %collective-permute-start.23 = (bf16[256,256]{1,0:T(8,128)(2,1)S(1)}, bf16[256,256]{1,0:T(8,128)(2,1)S(1)}, u32[]{:S(2)}, u32[]{:S(2)}) collective-permute-start(bf16[256,256]{1,0:T(8,128)(2,1)S(1)} %combine.22), channel_id=1, source_target_pairs={{0,8},{1,9},{2,10},{3,11},{4,12},{5,13},{6,14},{7,15},{8,0},{9,1},... | collective-permute-start | bytes 393224 | tf_op jit(solution)/shard_map/ppermute | solution.py:31
  69.5 11.2 %all-to-all-start = ((f32[32,8,128]{2,1,0:T(8,128)}), f32[32,8,128]{2,1,0:T(8,128)S(1)}, u32[]{:S(2)}, u32[]{:S(2)}) async-start(f32[32,8,128]{2,1,0:T(8,128)} %get-tuple-element.80), calls=%async_computation | async-start | bytes 262144 | tf_op jit(solution)/shard_map/all_to_all | solution.py:533
  (15 other events, 193.3 us)
